TPU v7x, 256 devices: a whole 4x4x8 slice. The times are simulated.
256 devices in a mesh: tau: 32 (over z, x), ka: 8 (over y, core).
Axes of the slice: x: 4, y: 4, z: 8, core: 2. Of those that a mesh axis runs over, the one named last changes fastest.
Arguments:
- green_times: bfloat16 [32, 96, 256, 256], P('tau', 'ka'), may hold values from -16 to 16
- screened: bfloat16 [32, 96, 256, 256], P('tau', None, 'ka'), may hold values from -0.01953125 to 0.01953125
- bare_green: bfloat16 [32, 96, 2, 256, 256], P('tau', 'ka'), may hold values from -6 to 6
Outputs:
- mixed_green: bfloat16 [32, 96, 256, 256], P('tau', 'ka')
All inputs are finite; a program needn't handle non-finite values.
Results may differ from a plain program's by a relative error of at most 0.025.
Values may be sent and summed in bfloat16 or wider, within the bound.
A program may use at most 128 MiB of HBM per device.

v0:
```python
import math

import jax
import jax.numpy as jnp
from jax import lax
from jax.sharding import PartitionSpec as P

KX = 6
KY = 4
KZ = 4
TURNS = 2


def hartley_table():
    count = KX * KY * KZ
    position = jnp.arange(count, dtype=jnp.int32)
    digit_one = position // (KY * KZ)
    digit_two = position // KZ % KY
    digit_three = position % KZ
    phase = (
        digit_one[:, None] * digit_one[None, :] * (KY * KZ)
        + digit_two[:, None] * digit_two[None, :] * (KX * KZ)
        + digit_three[:, None] * digit_three[None, :] * (KX * KY)
    ) % count
    angle = phase.astype(jnp.float32) * (2.0 * math.pi / count)
    return ((jnp.cos(angle) + jnp.sin(angle)) / math.sqrt(count)).astype(jnp.bfloat16)


def time_tables(points):
    position = jnp.arange(points, dtype=jnp.int32)
    odd_index = 2 * position + 1
    phase = odd_index[:, None] * odd_index[None, :] % (4 * points)
    angle = phase.astype(jnp.float32) * (math.pi / (2 * points))
    factor = 1.0 / math.sqrt(points)
    return jnp.stack([jnp.cos(angle) * factor, jnp.sin(angle) * factor]).astype(jnp.bfloat16)


def product(left, right):
    return jnp.einsum("nkab,nkbc->nkac", left, right, preferred_element_type=jnp.float32)


def per_device(green_times, screened, bare_green):
    tau_dev = green_times.shape[0]
    points = lax.axis_size("tau") * tau_dev
    total = float(
        points
        * green_times.shape[1]
        * lax.axis_size("ka")
        * green_times.shape[2]
        * green_times.shape[3]
    )
    lattice = hartley_table()
    weights = time_tables(points)
    bare_real = bare_green[:, :, 0]
    bare_imag = bare_green[:, :, 1]

    def to_freq(block):
        return jnp.einsum(
            "pnt,tkrc->nkprc", weights, block, preferred_element_type=jnp.float32
        ).astype(jnp.bfloat16)

    def to_time(block):
        return jnp.einsum(
            "pnt,nkprc->tkrc", weights, block, preferred_element_type=jnp.float32
        ).astype(jnp.bfloat16)

    def lattice_step(spread):
        cells = jnp.einsum("rk,tkac->trac", lattice, spread, preferred_element_type=jnp.float32)
        sigma_cells = (-cells * screened.astype(jnp.float32)).astype(jnp.bfloat16)
        return jnp.einsum(
            "kr,trac->tkac", lattice, sigma_cells, preferred_element_type=jnp.float32
        ).astype(jnp.bfloat16)

    def dyson(sigma_freq):
        sigma_real = sigma_freq[:, :, 0]
        sigma_imag = sigma_freq[:, :, 1]
        kernel_real = (product(bare_real, sigma_real) - product(bare_imag, sigma_imag)).astype(
            jnp.bfloat16
        )
        kernel_imag = (product(bare_real, sigma_imag) + product(bare_imag, sigma_real)).astype(
            jnp.bfloat16
        )
        dressed_real, dressed_imag = (bare_real, bare_imag)
        for turn in range(TURNS):
            new_real = (
                bare_real.astype(jnp.float32)
                + product(kernel_real, dressed_real)
                - product(kernel_imag, dressed_imag)
            )
            new_imag = (
                bare_imag.astype(jnp.float32)
                + product(kernel_real, dressed_imag)
                + product(kernel_imag, dressed_real)
            )
            dressed_real, dressed_imag = (
                new_real.astype(jnp.bfloat16),
                new_imag.astype(jnp.bfloat16),
            )
        return jnp.stack([dressed_real, dressed_imag], axis=2)

    def iterate_home(current):
        spread = lax.all_to_all(current, "ka", split_axis=2, concat_axis=1, tiled=True)
        sigma_lattice = lattice_step(spread)
        sigma_times = lax.all_to_all(sigma_lattice, "ka", split_axis=1, concat_axis=2, tiled=True)
        spread_freq = to_freq(
            lax.all_to_all(sigma_times, "tau", split_axis=2, concat_axis=0, tiled=True)
        )
        sigma_freq = lax.all_to_all(spread_freq, "tau", split_axis=0, concat_axis=3, tiled=True)
        dressed = dyson(sigma_freq)
        spread_time = to_time(
            lax.all_to_all(dressed, "tau", split_axis=3, concat_axis=0, tiled=True)
        )
        return lax.all_to_all(spread_time, "tau", split_axis=0, concat_axis=2, tiled=True)

    first_out = iterate_home(green_times)
    start = green_times.astype(jnp.float32)
    first_res = first_out.astype(jnp.float32) - start
    relaxed = ((start + first_out.astype(jnp.float32)) * 0.5).astype(jnp.bfloat16)
    second_out = iterate_home(relaxed)
    second_res = second_out.astype(jnp.float32) - relaxed.astype(jnp.float32)
    cross_local = jnp.sum(first_res * second_res)
    last_local = jnp.sum(second_res * second_res)
    first_sum, cross_sum, last_sum = lax.psum(
        (jnp.sum(first_res * first_res), cross_local, last_local), ("tau", "ka")
    )
    first_mean = first_sum / total
    cross_mean = cross_sum / total
    last_mean = last_sum / total
    weight = (last_mean - cross_mean) / (first_mean - 2.0 * cross_mean + last_mean + 1e-06)
    mixed = (
        weight * first_out.astype(jnp.float32) + (1.0 - weight) * second_out.astype(jnp.float32)
    ).astype(jnp.bfloat16)
    return mixed


def solution(mesh):
    return jax.shard_map(
        per_device,
        mesh=mesh,
        in_specs=(
            P("tau", "ka", None, None),
            P("tau", None, "ka", None),
            P("tau", "ka", None, None, None),
        ),
        out_specs=P("tau", "ka", None, None),
        check_vma=False,
    )
```

profile of v0, /device:TPU:1, one launch (start us, length us, event | category | flops | bytes accessed | tf_op | source)
XLA Modules:
  0.0 773.0 jit_solution(12914017553533894676)
XLA Ops:
  0.0 3.7 copy.219
  3.7 6.7 all-to-all-start
  10.4 26.3 %all-to-all-done = bf16[1,12,256,256]{3,1,0,2:T(8,128)(2,1)S(1)} async-done(((bf16[1,12,256,256]{3,1,0,2:T(8,128)(2,1)}), bf16[1,12,256,256]{3,1,0,2:T(8,128)(2,1)S(1)}, u32[]{:S(2)}, u32[]{:S(2)}) %all-to-all-start) | async-done | bytes 1572896 | tf_op jit(solution)/shard_map/all_to_all | solution.py:102
  36.8 0.5 copy.220
  37.4 4.5 fusion.75
  41.9 0.9 copy.224
  42.8 24.1 %all_to_all.192 = bf16[1,96,32,256]{3,2,0,1:T(8,128)(2,1)S(1)} all-to-all(bf16[1,96,32,256]{3,2,0,1:T(8,128)(2,1)S(1)} %copy.224), channel_id=1, replica_groups=mesh['tau'=32,'ka'=8] {'ka'}, dimensions={1} | all-to-all | bytes 3145728 | tf_op jit(solution)/shard_map/all_to_all | solution.py:104
  67.0 2.3 copy.226
  69.3 10.5 %all-to-all-start.2 = ((bf16[1,12,256,256]{3,1,0,2:T(8,128)(2,1)}), bf16[1,12,256,256]{3,1,0,2:T(8,128)(2,1)S(1)}, u32[]{:S(2)}, u32[]{:S(2)}) async-start(bf16[1,12,256,256]{3,1,0,2:T(8,128)(2,1)} %copy.226), calls=%async_computation.2 | async-start | bytes 4194304 | tf_op jit(solution)/shard_map/all_to_all | solution.py:106
  80.1 48.0 %all-to-all-done.2 = bf16[1,12,256,256]{3,1,0,2:T(8,128)(2,1)S(1)} async-done(((bf16[1,12,256,256]{3,1,0,2:T(8,128)(2,1)}), bf16[1,12,256,256]{3,1,0,2:T(8,128)(2,1)S(1)}, u32[]{:S(2)}, u32[]{:S(2)}) %all-to-all-start.2) | async-done | bytes 1572896 | tf_op jit(solution)/shard_map/all_to_all | solution.py:106
  128.0 2.8 convert_bitcast_fusion.1
  130.9 3.2 copy.229
  134.1 75.6 %all_to_all.193 = bf16[32,12,2,8,256]{4,2,3,1,0:T(2,128)(2,1)S(1)} all-to-all(bf16[32,12,2,8,256]{4,2,3,1,0:T(2,128)(2,1)S(1)} %copy.229), channel_id=1, replica_groups=mesh['tau'=32,'ka'=8] {'tau'}, dimensions={0} | all-to-all | bytes 6291456 | tf_op jit(solution)/shard_map/all_to_all | solution.py:108
  210.2 1.4 copy-done
  211.6 0.6 fusion.50
  212.2 0.6 fusion.54
  212.9 0.6 subtract_convert_fusion.1
  213.5 0.6 fusion.52
  214.1 0.6 fusion.37
  214.8 0.6 add_convert_fusion.1
  215.4 0.7 fusion.5
  216.2 0.7 fusion.13
  216.9 0.6 fusion.138
  217.6 0.6 fusion.137
  218.2 0.8 fusion.81
  219.0 0.7 fusion.83
  220.0 3.4 copy.242
  223.4 76.6 %all_to_all.194 = bf16[1,12,2,256,256]{4,2,1,0,3:T(2,128)(2,1)S(1)} all-to-all(bf16[1,12,2,256,256]{4,2,1,0,3:T(2,128)(2,1)S(1)} %copy.242), channel_id=1, replica_groups=mesh['tau'=32,'ka'=8] {'tau'}, dimensions={3} | all-to-all | bytes 6291456 | tf_op jit(solution)/shard_map/all_to_all | solution.py:111
  300.0 2.3 bitcast_convert_fusion.1
  302.3 0.9 copy.246
  303.2 42.5 %all_to_all.195 = bf16[32,12,8,256]{3,2,1,0:T(8,128)(2,1)S(1)} all-to-all(bf16[32,12,8,256]{3,2,1,0:T(8,128)(2,1)S(1)} %copy.246), channel_id=1, replica_groups=mesh['tau'=32,'ka'=8] {'tau'}, dimensions={0} | all-to-all | bytes 3145728 | tf_op jit(solution)/shard_map/all_to_all | solution.py:113
  345.7 0.5 fusion.1
  346.2 0.6 copy-done.1
  346.8 1.0 copy.248
  347.8 35.7 %all_to_all.196 = bf16[1,12,256,256]{3,1,0,2:T(8,128)(2,1)S(1)} all-to-all(bf16[1,12,256,256]{3,1,0,2:T(8,128)(2,1)S(1)} %copy.248), channel_id=1, replica_groups=mesh['tau'=32,'ka'=8] {'ka'}, dimensions={2} | all-to-all | bytes 3145728 | tf_op jit(solution)/shard_map/all_to_all | solution.py:102
  384.0 1.3 copy.250
  385.3 6.0 fusion.66
  391.4 2.3 copy.252
  393.6 24.2 %all_to_all.197 = bf16[1,96,32,256]{3,2,0,1:T(8,128)(2,1)S(1)} all-to-all(bf16[1,96,32,256]{3,2,0,1:T(8,128)(2,1)S(1)} %copy.252), channel_id=1, replica_groups=mesh['tau'=32,'ka'=8] {'ka'}, dimensions={1} | all-to-all | bytes 3145728 | tf_op jit(solution)/shard_map/all_to_all | solution.py:104
  418.0 1.0 copy.254
  419.0 52.2 %all_to_all.198 = bf16[1,12,256,256]{3,1,0,2:T(8,128)(2,1)S(1)} all-to-all(bf16[1,12,256,256]{3,1,0,2:T(8,128)(2,1)S(1)} %copy.254), channel_id=1, replica_groups=mesh['tau'=32,'ka'=8] {'tau'}, dimensions={2} | all-to-all | bytes 3145728 | tf_op jit(solution)/shard_map/all_to_all | solution.py:106
  471.2 2.9 convert_bitcast_fusion
  474.1 3.2 copy.257
  477.3 75.9 %all_to_all.199 = bf16[32,12,2,8,256]{4,2,3,1,0:T(2,128)(2,1)S(1)} all-to-all(bf16[32,12,2,8,256]{4,2,3,1,0:T(2,128)(2,1)S(1)} %copy.257), channel_id=1, replica_groups=mesh['tau'=32,'ka'=8] {'tau'}, dimensions={0} | all-to-all | bytes 6291456 | tf_op jit(solution)/shard_map/all_to_all | solution.py:108
  553.7 0.6 fusion.43
  554.4 0.6 fusion.47
  555.0 0.6 subtract_convert_fusion
  555.7 0.6 fusion.45
  556.3 0.6 fusion.32
  556.9 0.6 add_convert_fusion
  557.6 0.7 fusion.9
  558.3 0.7 fusion.17
  559.1 0.6 fusion.140
  559.7 0.6 fusion.139
  560.4 0.8 fusion.80
  561.1 0.7 fusion.82
  562.2 3.4 copy.269
  565.6 76.5 %all_to_all.200 = bf16[1,12,2,256,256]{4,2,1,0,3:T(2,128)(2,1)S(1)} all-to-all(bf16[1,12,2,256,256]{4,2,1,0,3:T(2,128)(2,1)S(1)} %copy.269), channel_id=1, replica_groups=mesh['tau'=32,'ka'=8] {'tau'}, dimensions={3} | all-to-all | bytes 6291456 | tf_op jit(solution)/shard_map/all_to_all | solution.py:111
  642.1 2.3 bitcast_convert_fusion
  644.3 0.9 copy.273
  645.2 43.2 %all_to_all.201 = bf16[32,12,8,256]{3,2,1,0:T(8,128)(2,1)S(1)} all-to-all(bf16[32,12,8,256]{3,2,1,0:T(8,128)(2,1)S(1)} %copy.273), channel_id=1, replica_groups=mesh['tau'=32,'ka'=8] {'tau'}, dimensions={0} | all-to-all | bytes 3145728 | tf_op jit(solution)/shard_map/all_to_all | solution.py:113
  688.5 2.4 multiply_reduce_fusion.1
  690.9 77.6 %all-reduce = (f32[]{:T(128)}, f32[]{:T(128)}, f32[]{:T(128)}) all-reduce(f32[]{:T(128)} %get-tuple-element.6, f32[]{:T(128)} %get-tuple-element.5, f32[]{:T(128)} %get-tuple-element.7), channel_id=1, replica_groups=mesh['tau'=32,'ka'=8] {'tau','ka'}, use_global_device_ids=true, to_apply=%region_1.2 | all-reduce | flops 3 | bytes 24 | tf_op jit(solution)/shard_map/psum | solution.py:123
  771.1 1.7 fusion.25
  (20 shorter events, 2.7 us)
Async XLA Ops:
  3.7 33.1 %all-to-all-start = ((bf16[1,12,256,256]{3,1,0,2:T(8,128)(2,1)}), bf16[1,12,256,256]{3,1,0,2:T(8,128)(2,1)S(1)}, u32[]{:S(2)}, u32[]{:S(2)}) async-start(bf16[1,12,256,256]{3,1,0,2:T(8,128)(2,1)} %copy.219), calls=%async_computation | async-start | bytes 4194304 | tf_op jit(solution)/shard_map/all_to_all | solution.py:102
  69.3 58.7 %all-to-all-start.2 = ((bf16[1,12,256,256]{3,1,0,2:T(8,128)(2,1)}), bf16[1,12,256,256]{3,1,0,2:T(8,128)(2,1)S(1)}, u32[]{:S(2)}, u32[]{:S(2)}) async-start(bf16[1,12,256,256]{3,1,0,2:T(8,128)(2,1)} %copy.226), calls=%async_computation.2 | async-start | bytes 4194304 | tf_op jit(solution)/shard_map/all_to_all | solution.py:106
  209.7 1.9 copy-start
  303.2 42.5 %copy-start.3 = (bf16[1,12,256,256]{3,2,1,0:T(8,128)(2,1)S(1)}, bf16[1,12,256,256]{3,2,1,0:T(8,128)(2,1)}, u32[]{:S(2)}) copy-start(bf16[1,12,256,256]{3,2,1,0:T(8,128)(2,1)} %param.3) | copy-start | bytes 4718596
  345.7 1.2 copy-start.1
  645.2 43.3 %copy-start.2 = (bf16[32,12,8,256]{3,2,1,0:T(8,128)(2,1)S(1)}, bf16[32,12,8,256]{3,2,1,0:T(8,128)(2,1)}, u32[]{:S(2)}) copy-start(bf16[32,12,8,256]{3,2,1,0:T(8,128)(2,1)} %copy-done.1) | copy-start | bytes 4718596
  645.2 43.2 %copy-start.4 = (bf16[1,12,256,256]{3,2,1,0:T(8,128)(2,1)S(1)}, bf16[1,12,256,256]{3,2,1,0:T(8,128)(2,1)}, u32[]{:S(2)}) copy-start(bf16[1,12,256,256]{3,2,1,0:T(8,128)(2,1)} %param.3) | copy-start | bytes 4718596
where the time goes:
time: 779 us; the launch traced here: 773 us
  blocking collectives  604 us (78%)
  waiting for transfers between devices  74.3 us (10%)
  matrix products  36.9 us (5%)
  local copies, waits for them, and re-layouts  31.8 us (4%)
  starting transfers between devices  17.3 us (2%)
    all_to_all x2, blocking collectives, iterate_home(): lax.all_to_all(dressed, 'tau', split_axis=3, concat_axis=0, tiled=True)  153 us
    all_to_all x2, blocking collectives, iterate_home(): lax.all_to_all(spread_freq, 'tau', split_axis=0, concat_axis=3, tiled=True)  151 us
    all_to_all x2, blocking collectives, iterate_home(): lax.all_to_all(spread_time, 'tau', split_axis=0, concat_axis=2, tiled=True)  85.7 us
    psum x1, blocking collectives, per_device(): lax.psum((jnp.sum(first_res * first_res), cross_local, last_local), ('tau...  77.6 us
    all_to_all x1, blocking collectives, iterate_home(): lax.all_to_all(sigma_times, 'tau', split_axis=2, concat_axis=0, tiled=True)  52.2 us
    all_to_all x2, blocking collectives, iterate_home(): lax.all_to_all(sigma_lattice, 'ka', split_axis=1, concat_axis=2, tiled=True)  48.3 us
    all_to_all x1, waiting for transfers between devices, iterate_home(): lax.all_to_all(sigma_times, 'tau', split_axis=2, concat_axis=0, tiled=True)  48 us
    all_to_all x1, blocking collectives, iterate_home(): lax.all_to_all(current, 'ka', split_axis=2, concat_axis=1, tiled=True)  35.7 us
  transfers between devices with their start and end apart: 2, of which 2 were waited for; matrix products, arithmetic and copies ran while one was open for 0% of the time, Pallas kernels for 0%

commit v1 on v0

v1 whole, which is shorter than its diff:
```python
import math

import jax
import jax.numpy as jnp
import numpy as np
from jax import lax
from jax.sharding import PartitionSpec as P

KX = 6
KY = 4
KZ = 4
TURNS = 2
F32 = jnp.float32
BF16 = jnp.bfloat16


def hartley_table():
    count = KX * KY * KZ
    position = np.arange(count)
    one = position // (KY * KZ)
    two = position // KZ % KY
    three = position % KZ
    phase = (
        one[:, None] * one[None, :] * (KY * KZ)
        + two[:, None] * two[None, :] * (KX * KZ)
        + three[:, None] * three[None, :] * (KX * KY)
    ) % count
    angle = phase * (2.0 * math.pi / count)
    return (np.cos(angle) + np.sin(angle)) / math.sqrt(count)


def time_tables(points):
    odd = 2 * np.arange(points) + 1
    angle = (odd[:, None] * odd[None, :] % (4 * points)) * (math.pi / (2 * points))
    factor = 1.0 / math.sqrt(points)
    return np.stack([np.cos(angle) * factor, np.sin(angle) * factor])


def product(left, right):
    return jnp.einsum("kab,kbc->kac", left, right, preferred_element_type=F32)


def dyson(bare_real, bare_imag, sigma_real, sigma_imag):
    kernel_real = (product(bare_real, sigma_real) - product(bare_imag, sigma_imag)).astype(BF16)
    kernel_imag = (product(bare_real, sigma_imag) + product(bare_imag, sigma_real)).astype(BF16)
    dressed_real, dressed_imag = bare_real, bare_imag
    for turn in range(TURNS):
        new_real = (
            bare_real.astype(F32)
            + product(kernel_real, dressed_real)
            - product(kernel_imag, dressed_imag)
        )
        new_imag = (
            bare_imag.astype(F32)
            + product(kernel_real, dressed_imag)
            + product(kernel_imag, dressed_real)
        )
        if turn < TURNS - 1:
            dressed_real, dressed_imag = new_real.astype(BF16), new_imag.astype(BF16)
    return new_real, new_imag


def per_device(green_times, screened, bare_green):
    points = lax.axis_size("tau")
    parts = lax.axis_size("ka")
    _, own_k, rows, cols = green_times.shape
    half = own_k // 2
    sub = rows // parts
    count = own_k * parts
    me = lax.axis_index("tau")
    low = me < points // 2

    order = np.arange(count).reshape(parts, 2, half).swapaxes(0, 1).reshape(-1)
    lattice = hartley_table()
    to_cells = jnp.asarray(lattice[:, order], BF16)
    to_points = jnp.asarray(lattice[order, :], BF16)
    table = time_tables(points)
    tables = jnp.asarray(table.transpose(1, 0, 2).reshape(2, points, points), BF16)

    def to_rows(block):
        spread = lax.all_to_all(block, "ka", split_axis=2, concat_axis=1, tiled=True)
        spread = spread.reshape(count, sub, cols).swapaxes(0, 1)
        return lax.all_to_all(spread, "tau", split_axis=0, concat_axis=0, tiled=True)

    def to_home(block):
        spread = lax.all_to_all(block, "tau", split_axis=0, concat_axis=0, tiled=True)
        spread = spread.reshape(sub, 2, parts * half, cols).transpose(1, 2, 0, 3)
        return lax.all_to_all(spread, "ka", split_axis=1, concat_axis=2, tiled=True)

    own, other = bare_green[0], None
    keep = jnp.where(low, own[:half], own[half:])
    send = jnp.where(low, own[half:], own[:half])
    other = lax.ppermute(send, "tau", [(i, points - 1 - i) for i in range(points)])

    start = to_rows(green_times.reshape(2, half, rows, cols))
    screen = lax.all_to_all(
        screened[0].swapaxes(0, 1), "tau", split_axis=0, concat_axis=0, tiled=True
    )

    def iterate(current):
        cells = jnp.einsum("rk,tkc->trc", to_cells, current, preferred_element_type=F32)
        sigma_cells = (-cells * screen.astype(F32)).astype(BF16)
        sigma = jnp.einsum(
            "kr,trc->tkc", to_points, sigma_cells, preferred_element_type=F32
        ).astype(BF16)
        sigma = sigma.reshape(points, 2, count // 2, cols)
        freq = jnp.einsum("hqt,thkc->hqkc", tables, sigma, preferred_element_type=F32).astype(BF16)
        freq = to_home(freq.reshape(points, count, cols))
        own_real, own_imag = dyson(keep[:, 0], keep[:, 1], freq[0], freq[1])
        other_real, other_imag = dyson(other[:, 0], other[:, 1], -freq[0], freq[1])
        dressed = jnp.stack([own_real - other_real, own_imag + other_imag]).astype(BF16)
        dressed = to_rows(dressed).reshape(2, points, count // 2, cols)
        back = jnp.einsum("hqt,hqkc->thkc", tables, dressed, preferred_element_type=F32)
        return back.astype(BF16).reshape(points, count, cols)

    first = iterate(start)
    begin = start.astype(F32)
    first_res = first.astype(F32) - begin
    relaxed = ((begin + first.astype(F32)) * 0.5).astype(BF16)
    second = iterate(relaxed)
    second_res = second.astype(F32) - relaxed.astype(F32)
    sums = jnp.stack(
        [
            jnp.sum(first_res * first_res),
            jnp.sum(first_res * second_res),
            jnp.sum(second_res * second_res),
        ]
    )
    total = float(points * count * rows * cols)
    means = lax.psum(sums, ("tau", "ka")) / total
    weight = (means[2] - means[1]) / (means[0] - 2.0 * means[1] + means[2] + 1e-06)
    mixed = (weight * first.astype(F32) + (1.0 - weight) * second.astype(F32)).astype(BF16)
    return to_home(mixed).reshape(1, own_k, rows, cols)


def solution(mesh):
    return jax.shard_map(
        per_device,
        mesh=mesh,
        in_specs=(
            P("tau", "ka", None, None),
            P("tau", None, "ka", None),
            P("tau", "ka", None, None, None),
        ),
        out_specs=P("tau", "ka", None, None),
        check_vma=False,
    )
```

time: 779 us -> 668 us (0.86)
  blocking collectives: 604 us -> 436 us
  waiting for transfers between devices: 74.3 us -> 120 us
  starting transfers between devices: 17.3 us -> 26.5 us
    all_to_all x10, blocking collectives: 526 us -> 360 us  [the longest x3 130 us: to_home(): lax.all_to_all(block, 'tau', split_axis=0, concat_axis=0, tiled=True)]
    ppermute x0 -> x1, waiting for transfers between devices: none -> 47.5 us  [per_device(): lax.ppermute(send, 'tau', [(i, points - 1 - i) for i in range(points)])]
    reshape x0 -> x5, local copies, waits for them, and re-layouts: none -> 10.1 us  [the longest x1 4.2 us: per_device(): start = to_rows(green_times.reshape(2, half, rows, cols))]
    all_to_all x2 -> x3, starting transfers between devices: 17.3 us -> 26 us  [the longest x1 10.3 us: per_device(): lax.all_to_all(screened[0].swapaxes(0, 1), 'tau', split_axis=0, concat_ax...]
    dot_general x30 -> x54, matrix products: 36.9 us -> 32.6 us  [the longest x48 20.2 us: product(): return jnp.einsum('kab,kbc->kac', left, right, preferred_element_type=F32)]
    all_to_all x2 -> x3, waiting for transfers between devices: 74.3 us -> 72.5 us  [the longest x1 35.1 us: per_device(): lax.all_to_all(screened[0].swapaxes(0, 1), 'tau', split_axis=0, concat_ax...]
  transfers between devices with their start and end apart: 2 -> 4, of which waited for: 2 -> 4; matrix products, arithmetic and copies ran while one was open for 0% -> 2% of each run, Pallas kernels for 0% -> 0%
where the time goes in v1:
time: 668 us; the launch traced here: 660 us
  blocking collectives  436 us (65%)
  waiting for transfers between devices  120 us (18%)
  matrix products  32.6 us (5%)
  local copies, waits for them, and re-layouts  30.8 us (5%)
  starting transfers between devices  26.5 us (4%)
  other arithmetic  9.74 us (1%)
    all_to_all x3, blocking collectives, to_home(): lax.all_to_all(block, 'tau', split_axis=0, concat_axis=0, tiled=True)  130 us
    all_to_all x3, blocking collectives, to_rows(): lax.all_to_all(spread, 'tau', split_axis=0, concat_axis=0, tiled=True)  127 us
    psum x1, blocking collectives, per_device(): means = lax.psum(sums, ('tau', 'ka')) / total  75.6 us
    all_to_all x2, blocking collectives, to_home(): return lax.all_to_all(spread, 'ka', split_axis=1, concat_axis=2, tiled=True)  53.2 us
    all_to_all x2, blocking collectives, to_rows(): lax.all_to_all(block, 'ka', split_axis=2, concat_axis=1, tiled=True)  50.2 us
    ppermute x1, waiting for transfers between devices, per_device(): lax.ppermute(send, 'tau', [(i, points - 1 - i) for i in range(points)])  47.5 us
    all_to_all x1, waiting for transfers between devices, per_device(): lax.all_to_all(screened[0].swapaxes(0, 1), 'tau', split_axis=0, concat_ax...  35.1 us
    dot_general x48, matrix products, product(): return jnp.einsum('kab,kbc->kac', left, right, preferred_element_type=F32)  20.2 us
  transfers between devices with their start and end apart: 4, of which 4 were waited for; matrix products, arithmetic and copies ran while one was open for 2% of the time, Pallas kernels for 0%

profile of v1, /device:TPU:1, one launch (start us, length us, event | category | flops | bytes accessed | tf_op | source)
XLA Modules:
  0.0 659.7 jit_solution(16226854943610281551)
XLA Ops:
  0.0 4.2 copy.161
  4.2 6.9 %all-to-all-start = ((bf16[2,6,256,256]{3,0,1,2:T(2,128)(2,1)}), bf16[2,6,256,256]{3,0,1,2:T(2,128)(2,1)S(1)}, u32[]{:S(2)}, u32[]{:S(2)}) async-start(bf16[2,6,256,256]{3,0,1,2:T(2,128)(2,1)} %copy.161), calls=%async_computation | async-start | bytes 3145728 | tf_op jit(solution)/shard_map/all_to_all | solution.py:81
  11.1 2.0 copy.229
  13.1 18.7 %all-to-all-done = bf16[2,6,256,256]{3,0,1,2:T(2,128)(2,1)S(1)} async-done(((bf16[2,6,256,256]{3,0,1,2:T(2,128)(2,1)}), bf16[2,6,256,256]{3,0,1,2:T(2,128)(2,1)S(1)}, u32[]{:S(2)}, u32[]{:S(2)}) %all-to-all-start) | async-done | bytes 1572896 | tf_op jit(solution)/shard_map/all_to_all | solution.py:81
  31.8 10.3 %all-to-all-start.2 = ((bf16[32,96,256]{2,1,0:T(8,128)(2,1)}), bf16[32,96,256]{2,1,0:T(8,128)(2,1)S(1)}, u32[]{:S(2)}, u32[]{:S(2)}) async-start(bf16[32,96,256]{2,1,0:T(8,128)(2,1)} %bitcast.291), calls=%async_computation.2 | async-start | bytes 3145728 | tf_op jit(solution)/shard_map/all_to_all | solution.py:96
  42.5 2.1 copy.230
  44.5 35.1 %all-to-all-done.2 = bf16[32,96,256]{2,1,0:T(8,128)(2,1)S(1)} async-done(((bf16[32,96,256]{2,1,0:T(8,128)(2,1)}), bf16[32,96,256]{2,1,0:T(8,128)(2,1)S(1)}, u32[]{:S(2)}, u32[]{:S(2)}) %all-to-all-start.2) | async-done | bytes 1572896 | tf_op jit(solution)/shard_map/all_to_all | solution.py:96
  79.6 43.2 %all_to_all.125 = bf16[32,96,256]{2,1,0:T(8,128)(2,1)S(1)} all-to-all(bf16[32,96,256]{2,1,0:T(8,128)(2,1)} %bitcast.292), channel_id=1, replica_groups=mesh['tau'=32,'ka'=8] {'tau'}, dimensions={0} | all-to-all | bytes 3145728 | tf_op jit(solution)/shard_map/all_to_all | solution.py:83
  122.9 2.2 convolution_convert_fusion.3
  125.1 2.4 fusion.42
  127.5 0.9 copy.167
  128.4 43.2 %all_to_all.126 = bf16[32,96,256]{2,1,0:T(8,128)(2,1)S(1)} all-to-all(bf16[32,96,256]{2,1,0:T(8,128)(2,1)S(1)} %bitcast.297), channel_id=1, replica_groups=mesh['tau'=32,'ka'=8] {'tau'}, dimensions={0} | all-to-all | bytes 3145728 | tf_op jit(solution)/shard_map/all_to_all | solution.py:86
  171.6 2.0 copy.228
  173.7 8.9 %all-to-all-start.4 = ((bf16[2,48,32,256]{3,2,0,1:T(8,128)(2,1)}), bf16[2,48,32,256]{3,2,0,1:T(8,128)(2,1)}, u32[]{:S(2)}, u32[]{:S(2)}) async-start(bf16[2,48,32,256]{3,2,0,1:T(8,128)(2,1)} %bitcast.272), calls=%async_computation.4 | async-start | bytes 3145728 | tf_op jit(solution)/shard_map/all_to_all | solution.py:88
  182.7 1.4 select_bitcast_fusion.1
  184.1 0.5 collective-permute-start
  184.6 18.7 %all-to-all-done.4 = bf16[2,48,32,256]{3,2,0,1:T(8,128)(2,1)} async-done(((bf16[2,48,32,256]{3,2,0,1:T(8,128)(2,1)}), bf16[2,48,32,256]{3,2,0,1:T(8,128)(2,1)}, u32[]{:S(2)}, u32[]{:S(2)}) %all-to-all-start.4) | async-done | bytes 1572896 | tf_op jit(solution)/shard_map/all_to_all | solution.py:88
  203.4 1.5 copy.169
  206.0 0.4 subtract_convert_fusion.3
  206.8 0.4 add_convert_fusion.3
  207.1 0.4 fusion.7
  208.7 0.4 fusion.17
  209.8 47.5 %collective-permute-done = bf16[6,2,256,256]{3,2,0,1:T(8,128)(2,1)S(1)} collective-permute-done((bf16[6,2,256,256]{3,2,0,1:T(8,128)(2,1)}, bf16[6,2,256,256]{3,2,0,1:T(8,128)(2,1)S(1)}, u32[]{:S(2)}, u32[]{:S(2)}) %collective-permute-start) | collective-permute-done | bytes 1572896 | tf_op jit(solution)/shard_map/ppermute | solution.py:93
  259.3 0.4 fusion.33
  260.8 0.4 fusion.27
  261.6 1.4 fusion.51
  263.1 1.6 copy.172
  264.8 26.0 %all_to_all.127 = bf16[2,6,256,256]{3,0,1,2:T(2,128)(2,1)S(1)} all-to-all(bf16[2,6,256,256]{3,0,1,2:T(2,128)(2,1)S(1)} %copy.172), channel_id=1, replica_groups=mesh['tau'=32,'ka'=8] {'ka'}, dimensions={2} | all-to-all | bytes 3145728 | tf_op jit(solution)/shard_map/all_to_all | solution.py:81
  291.2 0.9 copy.175
  292.1 41.4 %all_to_all.128 = bf16[32,96,256]{2,1,0:T(8,128)(2,1)S(1)} all-to-all(bf16[32,96,256]{2,1,0:T(8,128)(2,1)S(1)} %copy.175), channel_id=1, replica_groups=mesh['tau'=32,'ka'=8] {'tau'}, dimensions={0} | all-to-all | bytes 3145728 | tf_op jit(solution)/shard_map/all_to_all | solution.py:83
  333.5 0.7 convert_bitcast_fusion.1
  334.2 1.8 copy.178
  336.0 1.6 copy-done
  337.7 1.7 fusion.3
  339.4 4.0 convolution_convert_fusion.1
  343.4 2.4 fusion.45
  345.9 0.9 copy.180
  346.8 43.1 %all_to_all.129 = bf16[32,96,256]{2,1,0:T(8,128)(2,1)S(1)} all-to-all(bf16[32,96,256]{2,1,0:T(8,128)(2,1)S(1)} %bitcast.301), channel_id=1, replica_groups=mesh['tau'=32,'ka'=8] {'tau'}, dimensions={0} | all-to-all | bytes 3145728 | tf_op jit(solution)/shard_map/all_to_all | solution.py:86
  389.9 0.9 copy.227
  390.8 27.3 %all_to_all.130 = bf16[2,48,32,256]{3,2,0,1:T(8,128)(2,1)S(1)} all-to-all(bf16[2,48,32,256]{3,2,0,1:T(8,128)(2,1)S(1)} %bitcast.303), channel_id=1, replica_groups=mesh['tau'=32,'ka'=8] {'ka'}, dimensions={1} | all-to-all | bytes 3145728 | tf_op jit(solution)/shard_map/all_to_all | solution.py:88
  420.4 0.4 add_convert_fusion.1
  420.8 0.4 fusion.12
  422.0 0.4 fusion.22
  423.9 0.4 add_convert_fusion
  425.1 0.4 fusion.36
  426.6 0.4 fusion.30
  427.4 1.4 fusion.50
  428.9 1.6 copy.185
  430.6 24.2 %all_to_all.131 = bf16[2,6,256,256]{3,0,1,2:T(2,128)(2,1)S(1)} all-to-all(bf16[2,6,256,256]{3,0,1,2:T(2,128)(2,1)S(1)} %copy.185), channel_id=1, replica_groups=mesh['tau'=32,'ka'=8] {'ka'}, dimensions={2} | all-to-all | bytes 3145728 | tf_op jit(solution)/shard_map/all_to_all | solution.py:81
  455.2 0.9 copy.188
  456.1 42.4 %all_to_all.132 = bf16[32,96,256]{2,1,0:T(8,128)(2,1)S(1)} all-to-all(bf16[32,96,256]{2,1,0:T(8,128)(2,1)S(1)} %copy.188), channel_id=1, replica_groups=mesh['tau'=32,'ka'=8] {'tau'}, dimensions={0} | all-to-all | bytes 3145728 | tf_op jit(solution)/shard_map/all_to_all | solution.py:83
  498.4 0.7 convert_bitcast_fusion
  499.2 1.8 copy.191
  501.0 0.5 copy-done.5
  501.5 0.5 copy-done.6
  502.0 1.8 multiply_reduce_fusion.2
  503.8 2.1 pad_maximum_fusion.2
  505.9 75.6 %psum.7 = f32[3]{0:T(128)S(1)} all-reduce(f32[3]{0:T(128)S(1)} %pad_maximum_fusion.2), channel_id=1, replica_groups=mesh['tau'=32,'ka'=8] {'tau','ka'}, use_global_device_ids=true, to_apply=%region_3.4 | all-reduce | flops 3 | bytes 24 | tf_op jit(solution)/shard_map/psum | solution.py:130
  581.4 0.7 fusion.79
  585.6 2.4 fusion.5
  588.0 43.3 %all_to_all.133 = bf16[32,96,256]{2,1,0:T(8,128)(2,1)S(1)} all-to-all(bf16[32,96,256]{2,1,0:T(8,128)(2,1)S(1)} %fusion.5), channel_id=1, replica_groups=mesh['tau'=32,'ka'=8] {'tau'}, dimensions={0} | all-to-all | bytes 3145728 | tf_op jit(solution)/shard_map/all_to_all | solution.py:86
  631.3 0.9 copy.226
  632.2 26.0 %all_to_all.134 = bf16[2,48,32,256]{3,2,0,1:T(8,128)(2,1)S(1)} all-to-all(bf16[2,48,32,256]{3,2,0,1:T(8,128)(2,1)S(1)} %bitcast.307), channel_id=1, replica_groups=mesh['tau'=32,'ka'=8] {'ka'}, dimensions={1} | all-to-all | bytes 3145728 | tf_op jit(solution)/shard_map/all_to_all | solution.py:88
  658.2 1.3 copy.194
  (74 shorter events, 15.2 us)
Async XLA Ops:
  4.2 6.9 %copy-start.9 = (bf16[1,96,32,256]{3,2,1,0:T(8,128)(2,1)S(1)}, bf16[1,96,32,256]{3,2,1,0:T(8,128)(2,1)}, u32[]{:S(2)}) copy-start(bf16[1,96,32,256]{3,2,1,0:T(8,128)(2,1)} %param.7) | copy-start | bytes 4718596
  4.2 27.6 %all-to-all-start = ((bf16[2,6,256,256]{3,0,1,2:T(2,128)(2,1)}), bf16[2,6,256,256]{3,0,1,2:T(2,128)(2,1)S(1)}, u32[]{:S(2)}, u32[]{:S(2)}) async-start(bf16[2,6,256,256]{3,0,1,2:T(2,128)(2,1)} %copy.161), calls=%async_computation | async-start | bytes 3145728 | tf_op jit(solution)/shard_map/all_to_all | solution.py:81
  31.8 47.8 %all-to-all-start.2 = ((bf16[32,96,256]{2,1,0:T(8,128)(2,1)}), bf16[32,96,256]{2,1,0:T(8,128)(2,1)S(1)}, u32[]{:S(2)}, u32[]{:S(2)}) async-start(bf16[32,96,256]{2,1,0:T(8,128)(2,1)} %bitcast.291), calls=%async_computation.2 | async-start | bytes 3145728 | tf_op jit(solution)/shard_map/all_to_all | solution.py:96
  79.6 43.2 %copy-start.7 = (bf16[32,96,256]{2,1,0:T(8,128)(2,1)}, bf16[32,96,256]{2,1,0:T(8,128)(2,1)S(1)}, u32[]{:S(2)}) copy-start(bf16[32,96,256]{2,1,0:T(8,128)(2,1)S(1)} %all-to-all-done.2) | copy-start | bytes 4718596
  79.6 43.2 %copy-start.11 = (bf16[96,96,1]{1,0,2:T(8,128)(2,1)S(1)}, bf16[96,96,1]{1,0,2:T(8,128)(2,1)}, u32[]{:S(2)}) copy-start(bf16[96,96,1]{1,0,2:T(8,128)(2,1)} %constant.34) | copy-start | bytes 55300
  79.6 43.2 %copy-start.12 = (bf16[96,96,1]{1,0,2:T(8,128)(2,1)S(1)}, bf16[96,96,1]{1,0,2:T(8,128)(2,1)}, u32[]{:S(2)}) copy-start(bf16[96,96,1]{1,0,2:T(8,128)(2,1)} %constant.33) | copy-start | bytes 55300
  122.9 2.2 copy-start.3
  122.9 2.2 copy-start.10
  173.7 8.9 %copy-start.8 = (bf16[1,12,2,256,256]{4,3,2,1,0:T(8,128)(2,1)S(1)}, bf16[1,12,2,256,256]{4,3,2,1,0:T(8,128)(2,1)}, u32[]{:S(2)}) copy-start(bf16[1,12,2,256,256]{4,3,2,1,0:T(8,128)(2,1)} %param.8) | copy-start | bytes 9437188
  173.7 29.7 %all-to-all-start.4 = ((bf16[2,48,32,256]{3,2,0,1:T(8,128)(2,1)}), bf16[2,48,32,256]{3,2,0,1:T(8,128)(2,1)}, u32[]{:S(2)}, u32[]{:S(2)}) async-start(bf16[2,48,32,256]{3,2,0,1:T(8,128)(2,1)} %bitcast.272), calls=%async_computation.4 | async-start | bytes 3145728 | tf_op jit(solution)/shard_map/all_to_all | solution.py:88
  184.1 73.2 %collective-permute-start = (bf16[6,2,256,256]{3,2,0,1:T(8,128)(2,1)}, bf16[6,2,256,256]{3,2,0,1:T(8,128)(2,1)S(1)}, u32[]{:S(2)}, u32[]{:S(2)}) collective-permute-start(bf16[6,2,256,256]{3,2,0,1:T(8,128)(2,1)} %get-tuple-element.13), channel_id=1, source_target_pairs={{0,248},{8,240},{16,232},{24,224},{32,216},{40,208},{48,200},{56,1... | collective-permute-start | bytes 4718600 | tf_op jit(solution)/shard_map/ppermute | solution.py:93
  334.2 3.5 copy-start.4
  336.0 1.7 copy-start
  499.1 1.9 copy-start.1
  499.1 2.3 copy-start.5
  499.1 2.8 copy-start.6
  502.0 1.8 copy-start.2

commit v2 on v1

v2 whole, which is shorter than its diff:
```python
import functools
import math

import jax
import jax.numpy as jnp
import numpy as np
from jax import lax
from jax.experimental import pallas as pl
from jax.experimental.pallas import tpu as pltpu
from jax.sharding import PartitionSpec as P

KX = 6
KY = 4
KZ = 4
TURNS = 2
F32 = jnp.float32
BF16 = jnp.bfloat16
MESH = pl.DeviceIdType.MESH

TAU = 32
KA = 8
NO = 256
SUB = NO // KA
CHUNKS = 3
PAIR = 2
GROUP = PAIR * KA
COUNT = KX * KY * KZ
VMEM = pltpu.VMEM
LIMIT = 56 << 20


def hartley_table():
    count = COUNT
    position = np.arange(count)
    one = position // (KY * KZ)
    two = position // KZ % KY
    three = position % KZ
    phase = (
        one[:, None] * one[None, :] * (KY * KZ)
        + two[:, None] * two[None, :] * (KX * KZ)
        + three[:, None] * three[None, :] * (KX * KY)
    ) % count
    angle = phase * (2.0 * math.pi / count)
    return (np.cos(angle) + np.sin(angle)) / math.sqrt(count)


def time_tables(points):
    odd = 2 * np.arange(points) + 1
    angle = (odd[:, None] * odd[None, :] % (4 * points)) * (math.pi / (2 * points))
    factor = 1.0 / math.sqrt(points)
    return np.stack([np.cos(angle) * factor, np.sin(angle) * factor])


def tables():
    order = np.arange(COUNT).reshape(KA, 2, CHUNKS, PAIR).transpose(2, 1, 3, 0).reshape(-1)
    lattice = hartley_table()
    to_cells = lattice[:, order]
    to_points = lattice[order, :]
    times = time_tables(TAU).transpose(1, 0, 2).reshape(2, TAU, TAU)
    eye = np.eye(GROUP)
    to_freq = np.stack([np.kron(times[h], eye) for h in range(2)])
    to_time = np.stack([np.kron(times[h].T, eye) for h in range(2)])
    swap = np.eye(256).reshape(16, 16, 256).swapaxes(0, 1).reshape(256, 256)
    return [jnp.asarray(v, BF16) for v in (to_cells, to_points, to_freq, to_time, swap)]


class Place:
    def __init__(self):
        self.t = lax.axis_index("tau")
        self.a = lax.axis_index("ka")

    def tau_peer(self, d):
        row = lax.rem(self.t // 4 + d // 4, 8)
        return row * 4 + lax.rem(lax.rem(self.t, 4) + lax.rem(d, 4), 4)

    def ka_peer(self, d):
        return lax.rem(self.a + d, KA)

    def barrier(self):
        sem = pltpu.get_barrier_semaphore()

        def greet_tau(d, c):
            pl.semaphore_signal(
                sem, inc=1, device_id=(self.tau_peer(d), self.a), device_id_type=MESH
            )
            return c

        def greet_ka(d, c):
            pl.semaphore_signal(
                sem, inc=1, device_id=(self.t, self.ka_peer(d)), device_id_type=MESH
            )
            return c

        lax.fori_loop(1, TAU, greet_tau, 0)
        lax.fori_loop(1, KA, greet_ka, 0)
        pl.semaphore_wait(sem, TAU - 1 + KA - 1)

    def tau_send(self, src, dst, sems):
        def step(d, c):
            n = self.tau_peer(d)
            pltpu.make_async_remote_copy(
                src_ref=src.at[n],
                dst_ref=dst.at[self.t],
                send_sem=sems.at[0],
                recv_sem=sems.at[1],
                device_id=(n, self.a),
                device_id_type=MESH,
            ).start()
            return c

        lax.fori_loop(1, TAU, step, 0)
        dst[self.t] = src[self.t]

    def ka_send(self, src_of, dst, sems):
        def step(d, c):
            b = self.ka_peer(d)
            pltpu.make_async_remote_copy(
                src_ref=src_of(b),
                dst_ref=dst,
                send_sem=sems.at[0],
                recv_sem=sems.at[1],
                device_id=(self.t, b),
                device_id_type=MESH,
            ).start()
            return c

        lax.fori_loop(1, KA, step, 0)


def take(ref, sem):
    pltpu.make_async_copy(ref, ref, sem).wait()


def turn_over(swap, block):
    flat = block.reshape(256, NO)
    return jnp.dot(swap[...], flat, preferred_element_type=F32).astype(BF16).reshape(16, 16, NO)


def spread_out(swap, held, staged):
    for part in range(2):
        for uh in range(SUB // 16):
            rows = pl.ds(uh * 16, 16)
            block = jnp.stack([held[b, part, i, rows, :] for i in range(PAIR) for b in range(KA)])
            staged[rows, part] = turn_over(swap, block)


def gather_in(swap, held, staged):
    for part in range(2):
        for uh in range(SUB // 16):
            rows = pl.ds(uh * 16, 16)
            block = turn_over(swap, held[rows, part])
            for i in range(PAIR):
                for b in range(KA):
                    staged[b, part, i, rows, :] = block[i * KA + b]


def block_rows(b):
    return pl.ds(pl.multiple_of(b * SUB, SUB), SUB)


def spread_kernel(x, screened, bare, swap, out_x, out_w, out_bare, held, staged_x, staged_w, sems, swap_sems):
    place = Place()
    t, a = place.t, place.a
    place.barrier()
    mine = t // (TAU // 2)
    exchange = pltpu.make_async_remote_copy(
        src_ref=bare.at[1 - mine],
        dst_ref=out_bare,
        send_sem=swap_sems.at[0],
        recv_sem=swap_sems.at[1],
        device_id=(TAU - 1 - t, a),
        device_id_type=MESH,
    )
    for q in range(CHUNKS):
        points = pl.ds(q * PAIR, PAIR)
        place.ka_send(
            lambda b: x.at[:, points, block_rows(b), :], held.at[q, a], sems.at[q]
        )
        held[q, a] = x[:, points, block_rows(a), :]
    exchange.start()
    for q in range(CHUNKS):
        for cb in range(2):
            for uh in range(SUB // 16):
                cells = pl.ds(q * 32 + cb * 16, 16)
                rows = pl.ds(uh * 16, 16)
                staged_w[q, rows, pl.ds(cb * 16, 16), :] = turn_over(swap, screened[cells, rows, :])
        place.tau_send(staged_w.at[q], out_w.at[q], sems.at[CHUNKS + q])
    for q in range(CHUNKS):
        take(held.at[q, pl.ds(0, KA - 1)], sems.at[q, 1])
        spread_out(swap, held.at[q], staged_x.at[q])
        place.tau_send(staged_x.at[q], out_x.at[q], sems.at[2 * CHUNKS + q])
    for q in range(CHUNKS):
        take(out_w.at[q, pl.ds(0, TAU - 1)], sems.at[CHUNKS + q, 1])
        take(out_x.at[q, pl.ds(0, TAU - 1)], sems.at[2 * CHUNKS + q, 1])
    for q in range(CHUNKS):
        take(held.at[q, pl.ds(0, KA - 1)], sems.at[q, 0])
        take(out_w.at[q, pl.ds(0, TAU - 1)], sems.at[CHUNKS + q, 0])
        take(out_x.at[q, pl.ds(0, TAU - 1)], sems.at[2 * CHUNKS + q, 0])
    exchange.wait()


def mul(left, right):
    return jnp.dot(left, right, preferred_element_type=F32)


def dyson(bare_real, bare_imag, kernel_real, kernel_imag):
    dressed_real, dressed_imag = bare_real, bare_imag
    for turn in range(TURNS):
        new_real = (
            bare_real.astype(F32) + mul(kernel_real, dressed_real) - mul(kernel_imag, dressed_imag)
        )
        new_imag = (
            bare_imag.astype(F32) + mul(kernel_real, dressed_imag) + mul(kernel_imag, dressed_real)
        )
        dressed_real, dressed_imag = new_real.astype(BF16), new_imag.astype(BF16)
    return new_real, new_imag


def round_kernel(
    x, w, bare, other, to_cells, to_points, to_freq, to_time, swap,
    out_y, out_next,
    sigma, freq, freq_rows, home_stage, home, dressed, back, back_stage, back_rows, sems,
):
    place = Place()
    t, a = place.t, place.a
    mine = t // (TAU // 2)

    def lattice(i, c):
        block = x[:, i].reshape(COUNT, NO)
        cells = mul(to_cells[...], block)
        sigma_cells = (-cells * w[:, i].reshape(COUNT, NO).astype(F32)).astype(BF16)
        sigma[:, i] = mul(to_points[...], sigma_cells).astype(BF16).reshape(CHUNKS, 2, GROUP, NO)
        return c

    lax.fori_loop(0, TAU, lattice, 0, unroll=4)
    place.barrier()

    for q in range(CHUNKS):
        for h in range(2):
            block = sigma[q, :, h].reshape(TAU * GROUP, NO)
            value = mul(to_freq[h], block).astype(BF16)
            freq[q, pl.ds(h * 16, 16)] = value.reshape(16, 2, GROUP, NO)
        place.tau_send(freq.at[q], freq_rows.at[q], sems.at[q])

    def to_home(q):
        take(freq_rows.at[q, pl.ds(0, TAU - 1)], sems.at[q, 1])
        gather_in(swap, freq_rows.at[q], home_stage.at[q])
        target = home.at[q, :, :, block_rows(a), :]
        place.ka_send(lambda b: home_stage.at[q, b], target, sems.at[CHUNKS + q])
        home[q, :, :, block_rows(a), :] = home_stage[q, a]

    def solve(q):
        take(home_stage.at[q, pl.ds(0, KA - 1)], sems.at[CHUNKS + q, 1])

        def one(i, c):
            real, imag = home[q, 0, i], home[q, 1, i]
            point = q * PAIR + i
            br, bi = bare[mine, point, 0], bare[mine, point, 1]
            kr = (mul(br, real) - mul(bi, imag)).astype(BF16)
            ki = (mul(br, imag) + mul(bi, real)).astype(BF16)
            own_real, own_imag = dyson(br, bi, kr, ki)
            br, bi = other[point, 0], other[point, 1]
            kr = (-(mul(br, real) + mul(bi, imag))).astype(BF16)
            ki = (mul(br, imag) - mul(bi, real)).astype(BF16)
            other_real, other_imag = dyson(br, bi, kr, ki)
            dressed[q, 0, i] = (own_real - other_real).astype(BF16)
            dressed[q, 1, i] = (own_imag + other_imag).astype(BF16)
            return c

        lax.fori_loop(0, PAIR, one, 0)
        place.ka_send(
            lambda b: dressed.at[q, :, :, block_rows(b), :],
            back.at[q, a],
            sems.at[2 * CHUNKS + q],
        )
        back[q, a] = dressed[q, :, :, block_rows(a), :]

    def to_rows(q):
        take(back.at[q, pl.ds(0, KA - 1)], sems.at[2 * CHUNKS + q, 1])
        spread_out(swap, back.at[q], back_stage.at[q])
        place.tau_send(back_stage.at[q], back_rows.at[q], sems.at[3 * CHUNKS + q])

    to_home(0)
    to_home(1)
    solve(0)
    to_home(2)
    to_rows(0)
    solve(1)
    to_rows(1)
    solve(2)
    to_rows(2)

    for q in range(CHUNKS):
        take(back_rows.at[q, pl.ds(0, TAU - 1)], sems.at[3 * CHUNKS + q, 1])
        for h in range(2):
            block = back_rows[q, pl.ds(h * 16, 16)].reshape(TAU * GROUP, NO)
            value = mul(to_time[h], block).astype(BF16).reshape(TAU, GROUP, NO)
            out_y[q, :, h] = value
            half = (x[q, :, h].astype(F32) + value.astype(F32)) * 0.5
            out_next[q, :, h] = half.astype(BF16)
    for q in range(CHUNKS):
        take(freq_rows.at[q, pl.ds(0, TAU - 1)], sems.at[q, 0])
        take(home_stage.at[q, pl.ds(0, KA - 1)], sems.at[CHUNKS + q, 0])
        take(back.at[q, pl.ds(0, KA - 1)], sems.at[2 * CHUNKS + q, 0])
        take(back_rows.at[q, pl.ds(0, TAU - 1)], sems.at[3 * CHUNKS + q, 0])


def finish_kernel(
    x0, y0, x1, y1, swap, out,
    sums, tau_sums, part_sums, ka_sums, mixed, mixed_rows, home_stage, sems, sum_sems,
):
    place = Place()
    t, a = place.t, place.a

    def residuals(i, c):
        begin, first = x0[:, i].astype(F32), y0[:, i].astype(F32)
        relaxed, second = x1[:, i].astype(F32), y1[:, i].astype(F32)
        r0 = (first - begin).reshape(COUNT // 8, 8, NO)
        r1 = (second - relaxed).reshape(COUNT // 8, 8, NO)
        return (
            c[0] + jnp.sum(r0 * r0, axis=0),
            c[1] + jnp.sum(r0 * r1, axis=0),
            c[2] + jnp.sum(r1 * r1, axis=0),
        )

    zero = jnp.zeros((8, NO), F32)
    total = lax.fori_loop(0, TAU, residuals, (zero, zero, zero))
    sums[...] = jnp.stack([v[:, :128] + v[:, 128:] for v in total])
    place.barrier()

    def tau_step(d, c):
        pltpu.make_async_remote_copy(
            src_ref=sums,
            dst_ref=tau_sums.at[t],
            send_sem=sum_sems.at[0, 0],
            recv_sem=sum_sems.at[0, 1],
            device_id=(place.tau_peer(d), a),
            device_id_type=MESH,
        ).start()
        return c

    lax.fori_loop(1, TAU, tau_step, 0)
    tau_sums[t] = sums[...]
    take(tau_sums.at[pl.ds(0, TAU - 1)], sum_sems.at[0, 1])
    part_sums[...] = jnp.sum(tau_sums[...], axis=0)
    place.ka_send(lambda b: part_sums, ka_sums.at[a], sum_sems.at[1])
    ka_sums[a] = part_sums[...]
    take(ka_sums.at[pl.ds(0, KA - 1)], sum_sems.at[1, 1])
    whole = jnp.sum(ka_sums[...], axis=0)
    means = [jnp.sum(whole[j]) * (1.0 / (TAU * COUNT * NO * NO)) for j in range(3)]
    top = jnp.full((GROUP, NO), means[2] - means[1], F32)
    bottom = jnp.full((GROUP, NO), means[0] - 2.0 * means[1] + means[2] + 1e-06, F32)
    weight = top / bottom
    rest = 1.0 - weight

    for q in range(CHUNKS):

        def mix(i, c):
            value = weight * y0[q, i].astype(F32) + rest * y1[q, i].astype(F32)
            mixed[q, i] = value.astype(BF16)
            return c

        lax.fori_loop(0, TAU, mix, 0)
        place.tau_send(mixed.at[q], mixed_rows.at[q], sems.at[q])
    for q in range(CHUNKS):
        take(mixed_rows.at[q, pl.ds(0, TAU - 1)], sems.at[q, 1])
        gather_in(swap, mixed_rows.at[q], home_stage.at[q])
        points = pl.ds(q * PAIR, PAIR)
        place.ka_send(
            lambda b: home_stage.at[q, b],
            out.at[:, points, block_rows(a), :],
            sems.at[CHUNKS + q],
        )
        out[:, points, block_rows(a), :] = home_stage[q, a]
    for q in range(CHUNKS):
        take(home_stage.at[q, pl.ds(0, KA - 1)], sems.at[CHUNKS + q, 1])
    for q in range(CHUNKS):
        take(mixed_rows.at[q, pl.ds(0, TAU - 1)], sems.at[q, 0])
        take(home_stage.at[q, pl.ds(0, KA - 1)], sems.at[CHUNKS + q, 0])
    take(tau_sums.at[pl.ds(0, TAU - 1)], sum_sems.at[0, 0])
    take(ka_sums.at[pl.ds(0, KA - 1)], sum_sems.at[1, 0])


ROWS_X = (CHUNKS, TAU, 2, GROUP, NO)
ROWS_W = (CHUNKS, TAU, 2 * GROUP, NO)
HELD = (CHUNKS, KA, 2, PAIR, SUB, NO)
HOME = (CHUNKS, 2, PAIR, NO, NO)


def call(kernel, collective, outs, operands, scratch, anys=(), any_outs=()):
    place = lambda j, held: pl.BlockSpec(memory_space=pl.ANY if j in held else VMEM)
    return pl.pallas_call(
        kernel,
        out_shape=[jax.ShapeDtypeStruct(s, BF16) for s in outs],
        in_specs=[place(j, anys) for j in range(len(operands))],
        out_specs=[place(j, any_outs) for j in range(len(outs))],
        scratch_shapes=scratch,
        compiler_params=pltpu.CompilerParams(
            collective_id=collective, has_side_effects=True, vmem_limit_bytes=LIMIT
        ),
    )(*operands)


def per_device(green_times, screened, bare_green):
    to_cells, to_points, to_freq, to_time, swap = tables()
    half = CHUNKS * PAIR
    bare = bare_green.reshape(2, half, 2, NO, NO)
    buffer = lambda s: pltpu.VMEM(s, BF16)
    dma = pltpu.SemaphoreType.DMA
    x0, w, other = call(
        spread_kernel,
        0,
        [ROWS_X, ROWS_W, bare.shape[1:]],
        [green_times.reshape(2, half, NO, NO), screened[0], bare, swap],
        [buffer(HELD), buffer(ROWS_X), buffer(ROWS_W), dma((3 * CHUNKS, 2)), dma((2,))],
        anys=(2,),
        any_outs=(2,),
    )

    def one_round(x):
        return call(
            round_kernel,
            1,
            [ROWS_X, ROWS_X],
            [x, w, bare, other, to_cells, to_points, to_freq, to_time, swap],
            [
                buffer(ROWS_X), buffer(ROWS_X), buffer(ROWS_X), buffer(HELD), buffer(HOME),
                buffer(HOME), buffer(HELD), buffer(ROWS_X), buffer(ROWS_X), dma((4 * CHUNKS, 2)),
            ],
        )

    y0, x1 = one_round(x0)
    y1, _ = one_round(x1)
    (out,) = call(
        finish_kernel,
        2,
        [(2, half, NO, NO)],
        [x0, y0, x1, y1, swap],
        [
            pltpu.VMEM((3, 8, 128), F32), pltpu.VMEM((TAU, 3, 8, 128), F32),
            pltpu.VMEM((3, 8, 128), F32), pltpu.VMEM((KA, 3, 8, 128), F32),
            buffer(ROWS_X), buffer(ROWS_X), buffer(HELD), dma((2 * CHUNKS, 2)), dma((2, 2)),
        ],
    )
    return out.reshape(green_times.shape)


def solution(mesh):
    return jax.shard_map(
        per_device,
        mesh=mesh,
        in_specs=(
            P("tau", "ka", None, None),
            P("tau", None, "ka", None),
            P("tau", "ka", None, None, None),
        ),
        out_specs=P("tau", "ka", None, None),
        check_vma=False,
    )
```

time: 668 us -> 420 us (0.63); the launches traced: 660 us -> 420 us
  blocking collectives: 436 us -> 0 us
  Pallas kernels: 0 us -> 417 us
  waiting for transfers between devices: 120 us -> 0 us
  matrix products: 32.6 us -> 0 us
  local copies, waits for them, and re-layouts: 30.8 us -> 2.65 us
  starting transfers between devices: 26.5 us -> 0 us
  other arithmetic: 9.74 us -> 0 us
    pallas_call x0 -> x4, Pallas kernels: none -> 417 us  [call(): pl.pallas_call(kernel, out_shape=[jax.ShapeDtypeStruct(s, BF16) for s in...]
    all_to_all x10 -> x0, blocking collectives: 360 us -> none  [the longest x3 130 us: to_home(): lax.all_to_all(block, 'tau', split_axis=0, concat_axis=0, tiled=True)]
    psum x1 -> x0, blocking collectives: 75.6 us -> none  [per_device(): means = lax.psum(sums, ('tau', 'ka')) / total]
    all_to_all x3 -> x0, waiting for transfers between devices: 72.5 us -> none  [the longest x1 35.1 us: per_device(): lax.all_to_all(screened[0].swapaxes(0, 1), 'tau', split_axis=0, concat_ax...]
    ppermute x1 -> x0, waiting for transfers between devices: 47.5 us -> none  [per_device(): lax.ppermute(send, 'tau', [(i, points - 1 - i) for i in range(points)])]
    dot_general x54 -> x0, matrix products: 32.6 us -> none  [the longest x48 20.2 us: product(): return jnp.einsum('kab,kbc->kac', left, right, preferred_element_type=F32)]
    all_to_all x3 -> x0, starting transfers between devices: 26 us -> none  [the longest x1 10.3 us: per_device(): lax.all_to_all(screened[0].swapaxes(0, 1), 'tau', split_axis=0, concat_ax...]
    reshape x5 -> x0, local copies, waits for them, and re-layouts: 10.1 us -> none  [the longest x1 4.2 us: per_device(): start = to_rows(green_times.reshape(2, half, rows, cols))]
  transfers between devices with their start and end apart: 4 -> 0, of which waited for: 4 -> 0; matrix products, arithmetic and copies ran while one was open for 2% -> 0% of each run, Pallas kernels for 0% -> 0%
where the time goes in v2:
time: 420 us
  Pallas kernels  417 us (99%)
    pallas_call x4, Pallas kernels, call(): pl.pallas_call(kernel, out_shape=[jax.ShapeDtypeStruct(s, BF16) for s in...  417 us

profile of v2, /device:TPU:1, one launch (start us, length us, event | category | flops | bytes accessed | tf_op | source)
XLA Modules:
  0.0 419.9 jit_solution(11609309984670578426)
XLA Ops:
  0.0 149.1 %shard_map.82 = (bf16[3,32,2,16,256]{4,3,2,1,0:T(8,128)(2,1)}, bf16[3,32,32,256]{3,2,1,0:T(8,128)(2,1)}, bf16[6,2,256,256]{3,2,1,0:T(8,128)(2,1)}) custom-call(bf16[2,6,256,256]{3,2,1,0:T(8,128)(2,1)} %bitcast.8, bf16[96,32,256]{2,1,0:T(8,128)(2,1)} %bitcast.9, bf16[2,6,2,256,256]{4,3,2,1,0:T(8,128)(2,1)} %bitcast.4, bf16[256,256]{1,0:T(8,128)(2,1)} %constant.14.clone.swap), custom_call_target="tpu_custom_call" | custom-call | tf_op jit(solution)/shard_map/pallas_call | solution.py:392
  149.2 100.5 %shard_map.83 = (bf16[3,32,2,16,256]{4,3,2,1,0:T(8,128)(2,1)}, bf16[3,32,2,16,256]{4,3,2,1,0:T(8,128)(2,1)}) custom-call(bf16[3,32,2,16,256]{4,3,2,1,0:T(8,128)(2,1)} %get-tuple-element.11.x.x0, bf16[3,32,32,256]{3,2,1,0:T(8,128)(2,1)} %get-tuple-element.12.w, bf16[2,6,2,256,256]{4,3,2,1,0:T(8,128)(2,1)} %bitcast.5, ...), custom_call_target="tpu_custom_call" | custom-call | tf_op jit(solution)/shard_map/pallas_call | solution.py:392
  249.7 96.0 %shard_map.84 = (bf16[3,32,2,16,256]{4,3,2,1,0:T(8,128)(2,1)}, bf16[3,32,2,16,256]{4,3,2,1,0:T(8,128)(2,1)}) custom-call(bf16[3,32,2,16,256]{4,3,2,1,0:T(8,128)(2,1)} %get-tuple-element.15.x.x1, bf16[3,32,32,256]{3,2,1,0:T(8,128)(2,1)} %get-tuple-element.12.w, bf16[2,6,2,256,256]{4,3,2,1,0:T(8,128)(2,1)} %bitcast.6, ...), custom_call_target="tpu_custom_call" | custom-call | tf_op jit(solution)/shard_map/pallas_call | solution.py:392
  345.7 71.5 %shard_map.85 = bf16[2,6,256,256]{3,2,1,0:T(8,128)(2,1)} custom-call(bf16[3,32,2,16,256]{4,3,2,1,0:T(8,128)(2,1)} %get-tuple-element.11.x.x0, bf16[3,32,2,16,256]{4,3,2,1,0:T(8,128)(2,1)} %get-tuple-element.14.y0, bf16[3,32,2,16,256]{4,3,2,1,0:T(8,128)(2,1)} %get-tuple-element.15.x.x1, bf16[3,32,2,16,256]{4,3,2,1,0:T(8,128)(2,1)} %get-tuple-element.16.y1, ...), custom_call_target="tpu_custom_call" | custom-call | tf_op jit(solution)/shard_map/pallas_call | solution.py:392
  417.3 2.7 copy.10

commit v3 on v1

v3 whole, which is shorter than its diff:
```python
import math

import jax
import jax.numpy as jnp
import numpy as np
from jax import lax
from jax.experimental import pallas as pl
from jax.experimental.pallas import tpu as pltpu
from jax.sharding import PartitionSpec as P

KX = 6
KY = 4
KZ = 4
TURNS = 2
F32 = jnp.float32
BF16 = jnp.bfloat16
MESH = pl.DeviceIdType.MESH

Z, X, Y, C = 8, 4, 4, 2
TAU = Z * X
KA = Y * C
LAYER = X * KA
NO = 256
SUB = NO // KA
STEPS = 3
JUMP = 4
COUNT = KX * KY * KZ
VMEM = pltpu.VMEM
LIMIT = 60 << 20


def hartley_table():
    position = np.arange(COUNT)
    one = position // (KY * KZ)
    two = position // KZ % KY
    three = position % KZ
    phase = (
        one[:, None] * one[None, :] * (KY * KZ)
        + two[:, None] * two[None, :] * (KX * KZ)
        + three[:, None] * three[None, :] * (KX * KY)
    ) % COUNT
    angle = phase * (2.0 * math.pi / COUNT)
    return (np.cos(angle) + np.sin(angle)) / math.sqrt(COUNT)


def time_tables(points):
    odd = 2 * np.arange(points) + 1
    angle = (odd[:, None] * odd[None, :] % (4 * points)) * (math.pi / (2 * points))
    factor = 1.0 / math.sqrt(points)
    return np.stack([np.cos(angle) * factor, np.sin(angle) * factor])


def tables():
    order = np.arange(COUNT).reshape(Y, Z, STEPS).transpose(2, 1, 0).reshape(-1)
    lattice = hartley_table()
    to_cells = lattice[:, order]
    to_points = lattice[order, :]
    x, c, i = np.meshgrid(np.arange(X), np.arange(C), np.arange(2), indexing="ij")
    pairs = ((c + 2 * i) * X + x).reshape(-1)
    times = time_tables(TAU)[:, pairs, :]
    to_freq = np.einsum("pmt,kl,uv->kmputlv", times, np.eye(2), np.eye(8)).reshape(512, 512)
    swap = np.eye(256).reshape(16, 16, 256).swapaxes(0, 1).reshape(256, 256)
    leave = np.eye(256).reshape(2, 8, 16, 256).transpose(0, 2, 1, 3).reshape(256, 256)
    homing = np.eye(256).reshape(2, 16, 8, 256).transpose(1, 0, 2, 3).reshape(256, 256)
    arrays = (to_cells, to_points, to_freq, to_freq.T, swap, leave, leave.T, homing)
    return [jnp.asarray(v, BF16) for v in arrays]


def take(ref, sem):
    pltpu.make_async_copy(ref, ref, sem).wait()


def mul(left, right):
    return jnp.dot(left, right, preferred_element_type=F32)


def permute(matrix, block):
    return mul(matrix[...], block.reshape(256, NO)).astype(BF16).reshape(16, 16, NO)


def block_rows(b):
    return pl.ds(pl.multiple_of(b * SUB, SUB), SUB)


def dyson(bare_real, bare_imag, kernel_real, kernel_imag):
    dressed_real, dressed_imag = bare_real, bare_imag
    for turn in range(TURNS):
        new_real = (
            bare_real.astype(F32) + mul(kernel_real, dressed_real) - mul(kernel_imag, dressed_imag)
        )
        new_imag = (
            bare_imag.astype(F32) + mul(kernel_real, dressed_imag) + mul(kernel_imag, dressed_real)
        )
        dressed_real, dressed_imag = new_real.astype(BF16), new_imag.astype(BF16)
    return new_real, new_imag


def kernel(
    x_home, screened, bare, to_cells, to_points, to_freq, to_time, swap, leave, enter, homing,
    out,
    x_parts, x, w, y, sigma, sigma_out, sigma_in, freq_out, freq_in, dressed_out, dressed_in,
    time_out, time_in, home_out, home, bare_in, partial, sums, tau_sums, part_sums, ka_sums,
    x_sems, bare_sems, leave_sems, sigma_sems, freq_sems, dressed_sems, time_sems, home_sems, sum_sems,
):
    t, a = lax.axis_index("tau"), lax.axis_index("ka")
    my_z, my_x = t // X, lax.rem(t, X)
    my_y, my_c = a // C, lax.rem(a, C)

    def send(src, dst, sems, device):
        pltpu.make_async_remote_copy(
            src_ref=src, dst_ref=dst, send_sem=sems.at[0], recv_sem=sems.at[1],
            device_id=device, device_id_type=MESH,
        ).start()

    def loop(count, body):
        def step(d, c):
            body(d)
            return c

        lax.fori_loop(1, count, step, 0)

    def tau_peer(d):
        z, other_x = lax.rem(my_z + d // X, Z), lax.rem(my_x + lax.rem(d, X), X)
        return z, other_x, (z * X + other_x, a)

    def layer_peer(d):
        other_x, b = lax.rem(my_x + d // KA, X), lax.rem(a + lax.rem(d, KA), KA)
        return other_x, b, (my_z * X + other_x, b)

    def ka_peer(d):
        b = lax.rem(a + d, KA)
        return b, (t, b)

    low = my_z < Z // 2
    row = jnp.where(low, my_z, Z - 1 - my_z)
    goal_x = jnp.where(low, my_x, X - 1 - my_x)
    goal_i, goal_f = row // 2, jnp.where(low, 0, 1)
    goal_a = my_y * C + lax.rem(row, 2)

    def goal(jump):
        z = my_c * JUMP + jump
        here = (z == my_z) & (goal_x == my_x) & (goal_a == a)
        return here, (z * X + goal_x, goal_a)

    def origin(i, f):
        z = my_c + 2 * i if f == 0 else Z - 1 - (my_c + 2 * i)
        other_x = my_x if f == 0 else X - 1 - my_x
        b = my_y * C + my_z // JUMP
        here = (z == my_z) & (other_x == my_x) & (b == a)
        return here, (z * X + other_x, b)

    barrier = pltpu.get_barrier_semaphore()

    def greet(device):
        pl.semaphore_signal(barrier, inc=1, device_id=device, device_id_type=MESH)

    loop(TAU, lambda d: greet(tau_peer(d)[2]))
    loop(LAYER, lambda d: greet(layer_peer(d)[2]))
    for i in range(2):
        for f in range(2):
            here, device = origin(i, f)
            pl.when(jnp.logical_not(here))(lambda device=device: greet(device))
    greeters = TAU - 1 + LAYER - 1
    for jump in range(JUMP):
        greeters += jnp.where(goal(jump)[0], 0, 1)
    pl.semaphore_wait(barrier, greeters)

    for s in range(STEPS):

        def spread(d):
            b, device = ka_peer(d)
            send(x_home.at[:, s, block_rows(b), :], x_parts.at[s, a], x_sems.at[s], device)

        loop(KA, spread)
        x_parts[s, a] = x_home[:, s, block_rows(a), :]
    for s in range(STEPS):
        for jump in range(JUMP):
            here, device = goal(jump)
            arrived = bare_sems.at[s, goal_i, goal_f]
            target = bare_in.at[s, goal_i, goal_f]

            @pl.when(jnp.logical_not(here))
            def _():
                pltpu.make_async_remote_copy(
                    src_ref=bare.at[jump, s], dst_ref=target, send_sem=leave_sems.at[s, jump],
                    recv_sem=arrived, device_id=device, device_id_type=MESH,
                ).start()

            @pl.when(here)
            def _():
                pltpu.make_async_copy(bare.at[jump, s], target, arrived).start()

    for cells in range(COUNT // 16):
        for uh in range(2):
            rows, columns = pl.ds(uh * 16, 16), pl.ds(cells * 16, 16)
            w[rows, columns, :] = permute(swap, screened[columns, rows, :])
    for s in range(STEPS):
        take(x_parts.at[s, pl.ds(0, KA - 1)], x_sems.at[s, 1])
        for c in range(C):
            for uh in range(2):
                rows = pl.ds(uh * 16, 16)
                block = jnp.stack(
                    [x_parts[s, b * C + c, j, rows, :] for j in range(JUMP) for b in range(Y)]
                )
                x[0, s, rows, pl.ds(c * 16, 16), :] = permute(swap, block)

    def one_round(turn):
        def lattice(u, c):
            block = x[turn, :, u].reshape(COUNT, NO)
            cells = mul(to_cells[...], block)
            sigma_cells = (-cells * w[u].astype(F32)).astype(BF16)
            sigma[:, u] = mul(to_points[...], sigma_cells).astype(BF16).reshape(STEPS, 32, NO)
            return c

        lax.fori_loop(0, SUB, lattice, 0, unroll=4)
        if turn:
            for s in range(STEPS):
                take(sigma_in.at[0, s, pl.ds(0, TAU - 1)], sigma_sems.at[0, s, 0])
                take(freq_in.at[0, s, pl.ds(0, LAYER - 1)], freq_sems.at[0, s, 0])
                take(freq_in.at[0, s, pl.ds(0, LAYER - 1)], dressed_sems.at[0, s, 0])
                take(sigma_in.at[0, s, pl.ds(0, TAU - 1)], time_sems.at[0, s, 0])
                take(home_out.at[s, pl.ds(0, KA - 1)], home_sems.at[0, s, 0])

        for s in range(STEPS):
            for zh in range(2):
                for xh in range(2):
                    block = sigma[s, pl.ds(xh * 16, 16), pl.ds(zh * 16, 16), :]
                    block = permute(leave, block).reshape(2, 4, 2, 16, NO)
                    for j in range(2):
                        sigma_out[s, pl.ds(zh * 4, 4), xh * 2 + j] = block[j]

            def part(d):
                z, other_x, device = tau_peer(d)
                send(
                    sigma_out.at[s, z, other_x], sigma_in.at[turn, s, t],
                    sigma_sems.at[turn, s], device,
                )

            loop(TAU, part)
            sigma_in[turn, s, t] = sigma_out[s, my_z, my_x]

        def to_frequencies(s):
            take(sigma_in.at[turn, s, pl.ds(0, TAU - 1)], sigma_sems.at[turn, s, 1])
            for j in range(2):
                block = sigma_in[turn, s, :, j].reshape(512, NO)
                value = mul(to_freq[...], block).astype(BF16)
                freq_out[s, pl.ds(j * 2, 2)] = value.reshape(2, X * C, 2, 16, NO)

            def part(d):
                other_x, b, device = layer_peer(d)
                send(
                    freq_out.at[s, b // C, other_x * C + lax.rem(b, C)],
                    freq_in.at[turn, s, a * X + my_x],
                    freq_sems.at[turn, s], device,
                )

            loop(LAYER, part)
            freq_in[turn, s, a * X + my_x] = freq_out[s, my_y, my_x * C + my_c]

        def solve(s):
            take(freq_in.at[turn, s, pl.ds(0, LAYER - 1)], freq_sems.at[turn, s, 1])
            if turn == 0:
                for i in range(2):
                    for f in range(2):
                        take(bare_in.at[s, i, f], bare_sems.at[s, i, f])

            def one(i, c):
                both = freq_in[turn, s, :, i].astype(F32).reshape(LAYER, 2, 8, NO)
                real = both[:, 0].reshape(NO, NO).astype(BF16)
                imag = both[:, 1].reshape(NO, NO).astype(BF16)
                br, bi = bare_in[s, i, 0, 0], bare_in[s, i, 0, 1]
                kr = (mul(br, real) - mul(bi, imag)).astype(BF16)
                ki = (mul(br, imag) + mul(bi, real)).astype(BF16)
                low_real, low_imag = dyson(br, bi, kr, ki)
                br, bi = bare_in[s, i, 1, 0], bare_in[s, i, 1, 1]
                kr = (-(mul(br, real) + mul(bi, imag))).astype(BF16)
                ki = (mul(br, imag) - mul(bi, real)).astype(BF16)
                high_real, high_imag = dyson(br, bi, kr, ki)
                real = (low_real - high_real).reshape(LAYER, 1, 8, NO)
                imag = (low_imag + high_imag).reshape(LAYER, 1, 8, NO)
                both = jnp.concatenate([real, imag], axis=1).reshape(LAYER, 16, NO)
                dressed_out[s, :, i] = both.astype(BF16)
                return c

            lax.fori_loop(0, 2, one, 0)

            def part(d):
                other_x, b, device = layer_peer(d)
                send(
                    dressed_out.at[s, b * X + other_x],
                    dressed_in.at[turn, s, my_y, my_x * C + my_c],
                    dressed_sems.at[turn, s], device,
                )

            loop(LAYER, part)
            dressed_in[turn, s, my_y, my_x * C + my_c] = dressed_out[s, a * X + my_x]

        def to_times(s):
            take(freq_in.at[turn, s, pl.ds(0, LAYER - 1)], dressed_sems.at[turn, s, 1])
            for j in range(2):
                block = dressed_in[turn, s, pl.ds(j * 2, 2)].reshape(512, NO)
                value = mul(to_time[...], block).astype(BF16)
                time_out[s, :, j] = value.reshape(TAU, 16, NO)

            def part(d):
                z, other_x, device = tau_peer(d)
                send(
                    time_out.at[s, z * X + other_x], time_in.at[turn, s, my_z, my_x],
                    time_sems.at[turn, s], device,
                )

            loop(TAU, part)
            time_in[turn, s, my_z, my_x] = time_out[s, t]

        def finish(s):
            take(sigma_in.at[turn, s, pl.ds(0, TAU - 1)], time_sems.at[turn, s, 1])
            for zh in range(2):
                for xh in range(2):
                    rows, columns = pl.ds(xh * 16, 16), pl.ds(zh * 16, 16)
                    block = jnp.stack(
                        [time_in[turn, s, pl.ds(zh * 4, 4), xh * 2 + j] for j in range(2)]
                    )
                    value = permute(enter, block)
                    old = x[turn, s, rows, columns, :].astype(F32)
                    if turn == 0:
                        y[s, rows, columns, :] = value
                        x[1, s, rows, columns, :] = ((old + value.astype(F32)) * 0.5).astype(BF16)
                    else:
                        begin = x[0, s, rows, columns, :].astype(F32)
                        first = y[s, rows, columns, :].astype(F32) - begin
                        second = value.astype(F32) - old
                        for j, term in enumerate((first * first, first * second, second * second)):
                            partial[j] += jnp.sum(term.reshape(32, 8, NO), axis=0)
                    value = permute(homing, block)
                    for j in range(JUMP):
                        for b in range(Y):
                            home_out[s, b * C + zh, j, rows, :] = value[j * Y + b]

            def part(d):
                b, device = ka_peer(d)
                send(
                    home_out.at[s, b], home.at[turn, :, s, block_rows(a), :],
                    home_sems.at[turn, s], device,
                )

            loop(KA, part)
            home[turn, :, s, block_rows(a), :] = home_out[s, a]

        to_frequencies(0)
        to_frequencies(1)
        solve(0)
        to_frequencies(2)
        to_times(0)
        solve(1)
        to_times(1)
        solve(2)
        to_times(2)
        for s in range(STEPS):
            finish(s)

    partial[...] = jnp.zeros_like(partial)
    one_round(0)
    one_round(1)

    index = lax.broadcasted_iota(jnp.int32, (8, 128), 0)
    tile = jnp.zeros((8, 128), F32)
    for j in range(3):
        line = jnp.sum(partial[j], axis=0, keepdims=True)
        line = line[:, :128] + line[:, 128:]
        tile = jnp.where(index == j, jnp.broadcast_to(line, (8, 128)), tile)
    sums[...] = tile
    loop(TAU, lambda d: send(sums, tau_sums.at[t], sum_sems.at[0], tau_peer(d)[2]))
    tau_sums[t] = tile
    take(tau_sums.at[pl.ds(0, TAU - 1)], sum_sems.at[0, 1])
    part_sums[...] = jnp.sum(tau_sums[...], axis=0)
    loop(KA, lambda d: send(part_sums, ka_sums.at[a], sum_sems.at[1], ka_peer(d)[1]))
    ka_sums[a] = part_sums[...]
    take(ka_sums.at[pl.ds(0, KA - 1)], sum_sems.at[1, 1])
    whole = jnp.sum(ka_sums[...], axis=0)
    means = [
        jnp.sum(jnp.where(index == j, whole, 0.0)) * (1.0 / (TAU * COUNT * NO * NO))
        for j in range(3)
    ]
    top = jnp.full((NO, NO), means[2] - means[1], F32)
    weight = top / (means[0] - 2.0 * means[1] + means[2] + 1e-06)
    rest = 1.0 - weight
    for s in range(STEPS):
        for turn in range(2):
            take(home_out.at[s, pl.ds(0, KA - 1)], home_sems.at[turn, s, 1])
        for j in range(JUMP):
            value = weight * home[0, j, s].astype(F32) + rest * home[1, j, s].astype(F32)
            out[j, s] = value.astype(BF16)

    for s in range(STEPS):
        take(x_parts.at[s, pl.ds(0, KA - 1)], x_sems.at[s, 0])
        take(sigma_in.at[1, s, pl.ds(0, TAU - 1)], sigma_sems.at[1, s, 0])
        take(freq_in.at[1, s, pl.ds(0, LAYER - 1)], freq_sems.at[1, s, 0])
        take(freq_in.at[1, s, pl.ds(0, LAYER - 1)], dressed_sems.at[1, s, 0])
        take(sigma_in.at[1, s, pl.ds(0, TAU - 1)], time_sems.at[1, s, 0])
        take(home_out.at[s, pl.ds(0, KA - 1)], home_sems.at[1, s, 0])
        for jump in range(JUMP):
            here, _ = goal(jump)

            @pl.when(jnp.logical_not(here))
            def _():
                take(bare.at[jump, s], leave_sems.at[s, jump])

    take(tau_sums.at[pl.ds(0, TAU - 1)], sum_sems.at[0, 0])
    take(ka_sums.at[pl.ds(0, KA - 1)], sum_sems.at[1, 0])


def per_device(green_times, screened, bare_green):
    operands = [
        green_times.reshape(JUMP, STEPS, NO, NO),
        screened[0],
        bare_green.reshape(JUMP, STEPS, 2, NO, NO),
    ] + tables()
    buffer = lambda *s: pltpu.VMEM(s, BF16)
    floats = lambda *s: pltpu.VMEM(s, F32)
    dma = lambda *s: pltpu.SemaphoreType.DMA(s)
    whole = pl.BlockSpec(memory_space=VMEM)
    mixed = pl.pallas_call(
        kernel,
        out_shape=jax.ShapeDtypeStruct((JUMP, STEPS, NO, NO), BF16),
        in_specs=[whole, whole, pl.BlockSpec(memory_space=pl.ANY)] + [whole] * 8,
        out_specs=whole,
        scratch_shapes=[
            buffer(STEPS, KA, JUMP, SUB, NO),
            buffer(2, STEPS, SUB, 32, NO),
            buffer(SUB, COUNT, NO),
            buffer(STEPS, SUB, 32, NO),
            buffer(STEPS, SUB, 32, NO),
            buffer(STEPS, Z, X, 2, 16, NO),
            buffer(2, STEPS, TAU, 2, 16, NO),
            buffer(STEPS, Y, X * C, 2, 16, NO),
            buffer(2, STEPS, LAYER, 2, 16, NO),
            buffer(STEPS, LAYER, 2, 16, NO),
            buffer(2, STEPS, Y, X * C, 2, 16, NO),
            buffer(STEPS, TAU, 2, 16, NO),
            buffer(2, STEPS, Z, X, 2, 16, NO),
            buffer(STEPS, KA, JUMP, SUB, NO),
            buffer(2, JUMP, STEPS, NO, NO),
            buffer(STEPS, 2, 2, 2, NO, NO),
            floats(3, 8, NO),
            floats(8, 128),
            floats(TAU, 8, 128),
            floats(8, 128),
            floats(KA, 8, 128),
            dma(STEPS, 2),
            dma(STEPS, 2, 2),
            dma(STEPS, JUMP),
            dma(2, STEPS, 2),
            dma(2, STEPS, 2),
            dma(2, STEPS, 2),
            dma(2, STEPS, 2),
            dma(2, STEPS, 2),
            dma(2, 2),
        ],
        compiler_params=pltpu.CompilerParams(
            collective_id=0, has_side_effects=True, vmem_limit_bytes=LIMIT
        ),
    )(*operands)
    return mixed.reshape(green_times.shape)


def solution(mesh):
    return jax.shard_map(
        per_device,
        mesh=mesh,
        in_specs=(
            P("tau", "ka", None, None),
            P("tau", None, "ka", None),
            P("tau", "ka", None, None, None),
        ),
        out_specs=P("tau", "ka", None, None),
        check_vma=False,
    )
```

time: 668 us -> 305 us (0.46); the launches traced: 660 us -> 305 us
  blocking collectives: 436 us -> 0 us
  Pallas kernels: 0 us -> 302 us
  waiting for transfers between devices: 120 us -> 0 us
  matrix products: 32.6 us -> 0 us
  local copies, waits for them, and re-layouts: 30.8 us -> 2.65 us
  starting transfers between devices: 26.5 us -> 0 us
  other arithmetic: 9.74 us -> 0 us
    all_to_all x10 -> x0, blocking collectives: 360 us -> none  [the longest x3 130 us: to_home(): lax.all_to_all(block, 'tau', split_axis=0, concat_axis=0, tiled=True)]
    pallas_call x0 -> x1, Pallas kernels: none -> 302 us  [per_device(): pl.pallas_call(kernel, out_shape=jax.ShapeDtypeStruct((JUMP, STEPS, NO, N...]
    psum x1 -> x0, blocking collectives: 75.6 us -> none  [per_device(): means = lax.psum(sums, ('tau', 'ka')) / total]
    all_to_all x3 -> x0, waiting for transfers between devices: 72.5 us -> none  [the longest x1 35.1 us: per_device(): lax.all_to_all(screened[0].swapaxes(0, 1), 'tau', split_axis=0, concat_ax...]
    ppermute x1 -> x0, waiting for transfers between devices: 47.5 us -> none  [per_device(): lax.ppermute(send, 'tau', [(i, points - 1 - i) for i in range(points)])]
    dot_general x54 -> x0, matrix products: 32.6 us -> none  [the longest x48 20.2 us: product(): return jnp.einsum('kab,kbc->kac', left, right, preferred_element_type=F32)]
    all_to_all x3 -> x0, starting transfers between devices: 26 us -> none  [the longest x1 10.3 us: per_device(): lax.all_to_all(screened[0].swapaxes(0, 1), 'tau', split_axis=0, concat_ax...]
    reshape x5 -> x0, local copies, waits for them, and re-layouts: 10.1 us -> none  [the longest x1 4.2 us: per_device(): start = to_rows(green_times.reshape(2, half, rows, cols))]
  transfers between devices with their start and end apart: 4 -> 0, of which waited for: 4 -> 0; matrix products, arithmetic and copies ran while one was open for 2% -> 0% of each run, Pallas kernels for 0% -> 0%
where the time goes in v3:
time: 305 us
  Pallas kernels  302 us (99%)
    pallas_call x1, Pallas kernels, per_device(): pl.pallas_call(kernel, out_shape=jax.ShapeDtypeStruct((JUMP, STEPS, NO, N...  302 us

profile of v3, /device:TPU:1, one launch (start us, length us, event | category | flops | bytes accessed | tf_op | source)
XLA Modules:
  0.0 304.8 jit_solution(7734470822547791117)
XLA Ops:
  0.0 302.1 %shard_map.109 = bf16[4,3,256,256]{3,2,1,0:T(8,128)(2,1)} custom-call(bf16[4,3,256,256]{3,2,1,0:T(8,128)(2,1)} %bitcast.6, bf16[96,32,256]{2,1,0:T(8,128)(2,1)} %bitcast.7, bf16[4,3,2,256,256]{4,3,2,1,0:T(8,128)(2,1)} %bitcast.5, bf16[96,96]{1,0:T(8,128)(2,1)} %constant.16.clone.to_cells, bf16[96,96]{1,0:T(8,128)(2,1)} %constant.17.clone.to_points, ...), custom_call_target="tpu_custom_call" | custom-call | tf_op jit(solution)/shard_map/pallas_call | solution.py:422
  302.1 2.7 copy.13

commit v4 on v3

v4 whole, which is shorter than its diff:
```python
import math

import jax
import jax.numpy as jnp
import numpy as np
from jax import lax
from jax.experimental import pallas as pl
from jax.experimental.pallas import tpu as pltpu
from jax.sharding import PartitionSpec as P

KX = 6
KY = 4
KZ = 4
TURNS = 2
F32 = jnp.float32
BF16 = jnp.bfloat16
MESH = pl.DeviceIdType.MESH

Z, X, Y, C = 8, 4, 4, 2
TAU = Z * X
KA = Y * C
NO = 256
SUB = NO // KA
STEPS = 3
JUMP = 4
COUNT = KX * KY * KZ
VMEM = pltpu.VMEM
LIMIT = 60 << 20


def hartley_table():
    position = np.arange(COUNT)
    one = position // (KY * KZ)
    two = position // KZ % KY
    three = position % KZ
    phase = (
        one[:, None] * one[None, :] * (KY * KZ)
        + two[:, None] * two[None, :] * (KX * KZ)
        + three[:, None] * three[None, :] * (KX * KY)
    ) % COUNT
    angle = phase * (2.0 * math.pi / COUNT)
    return (np.cos(angle) + np.sin(angle)) / math.sqrt(COUNT)


def time_tables(points):
    odd = 2 * np.arange(points) + 1
    angle = (odd[:, None] * odd[None, :] % (4 * points)) * (math.pi / (2 * points))
    factor = 1.0 / math.sqrt(points)
    return np.stack([np.cos(angle) * factor, np.sin(angle) * factor])


def tables():
    s, z, x = np.meshgrid(np.arange(STEPS), np.arange(Z), np.arange(X), indexing="ij")
    j = z % JUMP
    order = (((x - j - s) % Y * C + z // JUMP) * JUMP + j) * STEPS + s
    lattice = hartley_table()
    to_cells = lattice[:, order.reshape(-1)]
    to_points = lattice[order.reshape(-1), :]
    x, c, i = np.meshgrid(np.arange(X), np.arange(C), np.arange(2), indexing="ij")
    pairs = ((c + 2 * i) * X + x).reshape(-1)
    times = time_tables(TAU)[:, pairs, :]
    to_freq = np.einsum("pmt,uv->mputv", times, np.eye(16)).reshape(512, 512)
    swap = np.eye(256).reshape(16, 16, 256).swapaxes(0, 1).reshape(256, 256)
    arrays = (to_cells, to_points, to_freq, to_freq.T, swap)
    return [jnp.asarray(v, BF16) for v in arrays]


def take(ref, sem):
    pltpu.make_async_copy(ref, ref, sem).wait()


def mul(left, right):
    return jnp.dot(left, right, preferred_element_type=F32)


def turn_over(swap, block):
    return mul(swap[...], block.reshape(256, NO)).astype(BF16).reshape(16, 16, NO)


def block_rows(b):
    return pl.ds(pl.multiple_of(b * SUB, SUB), SUB)


def dyson(bare_real, bare_imag, kernel_real, kernel_imag):
    dressed_real, dressed_imag = bare_real, bare_imag
    for turn in range(TURNS):
        new_real = (
            bare_real.astype(F32) + mul(kernel_real, dressed_real) - mul(kernel_imag, dressed_imag)
        )
        new_imag = (
            bare_imag.astype(F32) + mul(kernel_real, dressed_imag) + mul(kernel_imag, dressed_real)
        )
        dressed_real, dressed_imag = new_real.astype(BF16), new_imag.astype(BF16)
    return new_real, new_imag


def kernel(
    x_home, screened, bare, to_cells, to_points, to_freq, to_time, swap,
    out,
    x_parts, x, w, y, sigma, sigma_out, sigma_in, freq_out, freq_in, dressed_out, dressed_in,
    time_out, time_in, home, bare_in, partial, sums, tau_sums, part_sums, ka_sums,
    x_sems, bare_sems, leave_sems, sigma_sems, freq_sems, dressed_sems, time_sems, home_sems,
    sum_sems,
):
    t, a = lax.axis_index("tau"), lax.axis_index("ka")
    my_z, my_x = t // X, lax.rem(t, X)
    my_y, my_c = a // C, lax.rem(a, C)
    my_j = lax.rem(my_z, JUMP)
    my_rows = block_rows(a)

    def start(src, dst, send_sem, recv_sem, device):
        pltpu.make_async_remote_copy(
            src_ref=src, dst_ref=dst, send_sem=send_sem, recv_sem=recv_sem,
            device_id=device, device_id_type=MESH,
        ).start()

    def send(src, dst, sems, device):
        start(src, dst, sems.at[0], sems.at[1], device)

    def loop(count, body):
        def step(d, c):
            body(d)
            return c

        lax.fori_loop(1, count, step, 0)

    def tau_peer(d):
        turn = lax.rem(d, Z)
        far = jnp.where(lax.rem(turn, 2) == 1, (turn + 1) // 2, Z - turn // 2)
        z, other_x = lax.rem(my_z + far, Z), lax.rem(my_x + d // Z, X)
        return z * X + other_x, (z * X + other_x, a)

    def ka_peer(d):
        b = lax.rem(a + d, KA)
        return b, (t, b)

    low = my_z < Z // 2
    row = jnp.where(low, my_z, Z - 1 - my_z)
    column = jnp.where(low, my_x, X - 1 - my_x)
    goal_i, goal_f = row // 2, jnp.where(low, 0, 1)

    def goal(j, s):
        z, other_x = my_c * JUMP + j, lax.rem(my_y + j + s, X)
        b = lax.rem(column + j + s, Y) * C + lax.rem(row, 2)
        here = (z == my_z) & (other_x == my_x) & (b == a)
        return here, (z * X + other_x, b)

    def own_column(s):
        return lax.rem(my_y + 2 * Y - my_j - s, Y)

    def origin(i, f, s):
        z = my_c + 2 * i if f == 0 else Z - 1 - (my_c + 2 * i)
        other_x = own_column(s) if f == 0 else X - 1 - own_column(s)
        b = lax.rem(my_x + 2 * X - my_j - s, X) * C + my_z // JUMP
        here = (z == my_z) & (other_x == my_x) & (b == a)
        return here, (z * X + other_x, b)

    barrier = pltpu.get_barrier_semaphore()

    def greet(device):
        pl.semaphore_signal(barrier, inc=1, device_id=device, device_id_type=MESH)

    loop(TAU, lambda d: greet(tau_peer(d)[1]))
    loop(KA, lambda d: greet(ka_peer(d)[1]))
    greeters = TAU - 1 + KA - 1
    for s in range(STEPS):
        for i in range(2):
            for f in range(2):
                here, device = origin(i, f, s)
                pl.when(jnp.logical_not(here))(lambda device=device: greet(device))
        for j in range(JUMP):
            greeters += jnp.where(goal(j, s)[0], 0, 1)
    pl.semaphore_wait(barrier, greeters)

    for s in range(STEPS):

        def spread(d):
            b, device = ka_peer(d)
            send(x_home.at[:, s, block_rows(b), :], x_parts.at[s, a], x_sems.at[s], device)

        loop(KA, spread)
        x_parts[s, a] = x_home[:, s, my_rows, :]
    for s in range(STEPS):
        for j in range(JUMP):
            here, device = goal(j, s)
            arrived = bare_sems.at[s, goal_i, goal_f]
            target = bare_in.at[s, goal_i, goal_f]

            @pl.when(jnp.logical_not(here))
            def _():
                start(bare.at[j, s], target, leave_sems.at[s, j], arrived, device)

            @pl.when(here)
            def _():
                pltpu.make_async_copy(bare.at[j, s], target, arrived).start()

    for cells in range(COUNT // 16):
        for uh in range(2):
            rows, columns = pl.ds(uh * 16, 16), pl.ds(cells * 16, 16)
            w[rows, columns, :] = turn_over(swap, screened[columns, rows, :])
    for s in range(STEPS):
        take(x_parts.at[s, pl.ds(0, KA - 1)], x_sems.at[s, 1])
        for c in range(C):
            for uh in range(2):
                rows = pl.ds(uh * 16, 16)
                parts = [(j, (other_x - j - s) % Y) for j in range(JUMP) for other_x in range(X)]
                block = jnp.stack([x_parts[s, b * C + c, j, rows, :] for j, b in parts])
                x[0, s, rows, pl.ds(c * 16, 16), :] = turn_over(swap, block)

    def one_round(turn):
        def lattice(u, c):
            block = x[turn, :, u].reshape(COUNT, NO)
            cells = mul(to_cells[...], block)
            sigma_cells = (-cells * w[u].astype(F32)).astype(BF16)
            sigma[:, u] = mul(to_points[...], sigma_cells).astype(BF16).reshape(STEPS, TAU, NO)
            return c

        lax.fori_loop(0, SUB, lattice, 0, unroll=4)
        if turn:
            for s in range(STEPS):
                take(sigma_in.at[0, s, pl.ds(0, TAU - 1)], sigma_sems.at[0, s, 0])
                take(dressed_in.at[0, s, pl.ds(0, KA - 1)], freq_sems.at[0, s, 0])
                take(dressed_in.at[0, s, pl.ds(0, KA - 1)], dressed_sems.at[0, s, 0])
                take(sigma_in.at[0, s, pl.ds(0, TAU - 1)], time_sems.at[0, s, 0])

        for s in range(STEPS):
            for zh in range(2):
                for uh in range(2):
                    rows, points = pl.ds(uh * 16, 16), pl.ds(zh * 16, 16)
                    sigma_out[s, points, rows, :] = turn_over(swap, sigma[s, rows, points, :])

            def part(d):
                n, device = tau_peer(d)
                send(sigma_out.at[s, n], sigma_in.at[turn, s, t], sigma_sems.at[turn, s], device)

            loop(TAU, part)
            sigma_in[turn, s, t] = sigma_out[s, t]

        def to_frequencies(s):
            take(sigma_in.at[turn, s, pl.ds(0, TAU - 1)], sigma_sems.at[turn, s, 1])
            for uh in range(2):
                rows = pl.ds(uh * 16, 16)
                block = sigma_in[turn, s, :, rows, :].reshape(512, NO)
                value = mul(to_freq[...], block).astype(BF16)
                freq_out[s, :, :, :, rows, :] = value.reshape(KA, 2, 2, 16, NO)

            def place(b):
                return lax.rem(b // C + 2 * Y - my_j - s, Y) * C + lax.rem(b, C)

            def part(d):
                b, device = ka_peer(d)
                send(
                    freq_out.at[s, place(b)], freq_in.at[turn, s, :, :, my_rows, :],
                    freq_sems.at[turn, s], device,
                )

            loop(KA, part)
            freq_in[turn, s, :, :, my_rows, :] = freq_out[s, place(a)]

        def solve(s):
            take(dressed_in.at[turn, s, pl.ds(0, KA - 1)], freq_sems.at[turn, s, 1])
            if turn == 0:
                for i in range(2):
                    for f in range(2):
                        take(bare_in.at[s, i, f], bare_sems.at[s, i, f])

            def one(i, c):
                real, imag = freq_in[turn, s, i, 0], freq_in[turn, s, i, 1]
                br, bi = bare_in[s, i, 0, 0], bare_in[s, i, 0, 1]
                kr = (mul(br, real) - mul(bi, imag)).astype(BF16)
                ki = (mul(br, imag) + mul(bi, real)).astype(BF16)
                low_real, low_imag = dyson(br, bi, kr, ki)
                br, bi = bare_in[s, i, 1, 0], bare_in[s, i, 1, 1]
                kr = (-(mul(br, real) + mul(bi, imag))).astype(BF16)
                ki = (mul(br, imag) - mul(bi, real)).astype(BF16)
                high_real, high_imag = dyson(br, bi, kr, ki)
                dressed_out[s, i, 0] = (low_real - high_real).astype(BF16)
                dressed_out[s, i, 1] = (low_imag + high_imag).astype(BF16)
                return c

            lax.fori_loop(0, 2, one, 0)
            target = dressed_in.at[turn, s, own_column(s) * C + my_c]

            def part(d):
                b, device = ka_peer(d)
                send(
                    dressed_out.at[s, :, :, block_rows(b), :], target,
                    dressed_sems.at[turn, s], device,
                )

            loop(KA, part)
            dressed_in[turn, s, own_column(s) * C + my_c] = dressed_out[s, :, :, my_rows, :]

        def to_times(s):
            take(dressed_in.at[turn, s, pl.ds(0, KA - 1)], dressed_sems.at[turn, s, 1])
            for uh in range(2):
                rows = pl.ds(uh * 16, 16)
                block = dressed_in[turn, s, :, :, :, rows, :].reshape(512, NO)
                value = mul(to_time[...], block).astype(BF16)
                time_out[s, :, rows, :] = value.reshape(TAU, 16, NO)

            def part(d):
                n, device = tau_peer(d)
                send(time_out.at[s, n], time_in.at[turn, s, t], time_sems.at[turn, s], device)

            loop(TAU, part)
            time_in[turn, s, t] = time_out[s, t]

        def finish(s):
            take(sigma_in.at[turn, s, pl.ds(0, TAU - 1)], time_sems.at[turn, s, 1])

            def place(b, j):
                return (lax.rem(b, C) * JUMP + j) * X + lax.rem(b // C + j + s, X)

            def part(d):
                b, device = ka_peer(d)
                for j in range(JUMP):
                    send(
                        time_in.at[turn, s, place(b, j)], home.at[turn, j, s, my_rows, :],
                        home_sems.at[turn, s], device,
                    )

            loop(KA, part)
            for j in range(JUMP):
                home[turn, j, s, my_rows, :] = time_in[turn, s, place(a, j)]
            for zh in range(2):
                for uh in range(2):
                    rows, points = pl.ds(uh * 16, 16), pl.ds(zh * 16, 16)
                    value = turn_over(swap, time_in[turn, s, points, rows, :])
                    old = x[turn, s, rows, points, :].astype(F32)
                    if turn == 0:
                        y[s, rows, points, :] = value
                        x[1, s, rows, points, :] = ((old + value.astype(F32)) * 0.5).astype(BF16)
                    else:
                        begin = x[0, s, rows, points, :].astype(F32)
                        first = y[s, rows, points, :].astype(F32) - begin
                        second = value.astype(F32) - old
                        for j, term in enumerate((first * first, first * second, second * second)):
                            partial[j] += jnp.sum(term.reshape(32, 8, NO), axis=0)

        to_frequencies(0)
        to_frequencies(1)
        solve(0)
        to_frequencies(2)
        to_times(0)
        solve(1)
        to_times(1)
        solve(2)
        to_times(2)
        for s in range(STEPS):
            finish(s)

    partial[...] = jnp.zeros_like(partial)
    one_round(0)
    one_round(1)

    index = lax.broadcasted_iota(jnp.int32, (8, 128), 0)
    tile = jnp.zeros((8, 128), F32)
    for j in range(3):
        line = jnp.sum(partial[j], axis=0, keepdims=True)
        line = line[:, :128] + line[:, 128:]
        tile = jnp.where(index == j, jnp.broadcast_to(line, (8, 128)), tile)
    sums[...] = tile
    loop(TAU, lambda d: send(sums, tau_sums.at[t], sum_sems.at[0], tau_peer(d)[1]))
    tau_sums[t] = tile
    take(tau_sums.at[pl.ds(0, TAU - 1)], sum_sems.at[0, 1])
    part_sums[...] = jnp.sum(tau_sums[...], axis=0)
    loop(KA, lambda d: send(part_sums, ka_sums.at[a], sum_sems.at[1], ka_peer(d)[1]))
    ka_sums[a] = part_sums[...]
    take(ka_sums.at[pl.ds(0, KA - 1)], sum_sems.at[1, 1])
    whole = jnp.sum(ka_sums[...], axis=0)
    means = [
        jnp.sum(jnp.where(index == j, whole, 0.0)) * (1.0 / (TAU * COUNT * NO * NO))
        for j in range(3)
    ]
    top = jnp.full((NO, NO), means[2] - means[1], F32)
    weight = top / (means[0] - 2.0 * means[1] + means[2] + 1e-06)
    rest = 1.0 - weight
    for s in range(STEPS):
        for turn in range(2):
            take(x_parts.at[s, pl.ds(0, KA - 1)], home_sems.at[turn, s, 1])
        for j in range(JUMP):
            value = weight * home[0, j, s].astype(F32) + rest * home[1, j, s].astype(F32)
            out[j, s] = value.astype(BF16)

    for s in range(STEPS):
        take(x_parts.at[s, pl.ds(0, KA - 1)], x_sems.at[s, 0])
        take(sigma_in.at[1, s, pl.ds(0, TAU - 1)], sigma_sems.at[1, s, 0])
        take(dressed_in.at[1, s, pl.ds(0, KA - 1)], freq_sems.at[1, s, 0])
        take(dressed_in.at[1, s, pl.ds(0, KA - 1)], dressed_sems.at[1, s, 0])
        take(sigma_in.at[1, s, pl.ds(0, TAU - 1)], time_sems.at[1, s, 0])
        for turn in range(2):
            take(x_parts.at[s, pl.ds(0, KA - 1)], home_sems.at[turn, s, 0])
        for j in range(JUMP):

            @pl.when(jnp.logical_not(goal(j, s)[0]))
            def _():
                take(bare.at[j, s], leave_sems.at[s, j])

    take(tau_sums.at[pl.ds(0, TAU - 1)], sum_sems.at[0, 0])
    take(ka_sums.at[pl.ds(0, KA - 1)], sum_sems.at[1, 0])


def per_device(green_times, screened, bare_green):
    operands = [
        green_times.reshape(JUMP, STEPS, NO, NO),
        screened[0],
        bare_green.reshape(JUMP, STEPS, 2, NO, NO),
    ] + tables()
    buffer = lambda *s: pltpu.VMEM(s, BF16)
    floats = lambda *s: pltpu.VMEM(s, F32)
    dma = lambda *s: pltpu.SemaphoreType.DMA(s)
    whole = pl.BlockSpec(memory_space=VMEM)
    mixed = pl.pallas_call(
        kernel,
        out_shape=jax.ShapeDtypeStruct((JUMP, STEPS, NO, NO), BF16),
        in_specs=[whole, whole, pl.BlockSpec(memory_space=pl.ANY)] + [whole] * 5,
        out_specs=whole,
        scratch_shapes=[
            buffer(STEPS, KA, JUMP, SUB, NO),
            buffer(2, STEPS, SUB, TAU, NO),
            buffer(SUB, COUNT, NO),
            buffer(STEPS, SUB, TAU, NO),
            buffer(STEPS, SUB, TAU, NO),
            buffer(STEPS, TAU, SUB, NO),
            buffer(2, STEPS, TAU, SUB, NO),
            buffer(STEPS, KA, 2, 2, SUB, NO),
            buffer(2, STEPS, 2, 2, NO, NO),
            buffer(STEPS, 2, 2, NO, NO),
            buffer(2, STEPS, KA, 2, 2, SUB, NO),
            buffer(STEPS, TAU, SUB, NO),
            buffer(2, STEPS, TAU, SUB, NO),
            buffer(2, JUMP, STEPS, NO, NO),
            buffer(STEPS, 2, 2, 2, NO, NO),
            floats(3, 8, NO),
            floats(8, 128),
            floats(TAU, 8, 128),
            floats(8, 128),
            floats(KA, 8, 128),
            dma(STEPS, 2),
            dma(STEPS, 2, 2),
            dma(STEPS, JUMP),
            dma(2, STEPS, 2),
            dma(2, STEPS, 2),
            dma(2, STEPS, 2),
            dma(2, STEPS, 2),
            dma(2, STEPS, 2),
            dma(2, 2),
        ],
        compiler_params=pltpu.CompilerParams(
            collective_id=0, has_side_effects=True, vmem_limit_bytes=LIMIT
        ),
    )(*operands)
    return mixed.reshape(green_times.shape)


def solution(mesh):
    return jax.shard_map(
        per_device,
        mesh=mesh,
        in_specs=(
            P("tau", "ka", None, None),
            P("tau", None, "ka", None),
            P("tau", "ka", None, None, None),
        ),
        out_specs=P("tau", "ka", None, None),
        check_vma=False,
    )
```

time: 305 us -> 300 us (0.984)
  Pallas kernels: 302 us -> 298 us
    pallas_call x1, Pallas kernels: 302 us -> 298 us  [per_device(): pl.pallas_call(kernel, out_shape=jax.ShapeDtypeStruct((JUMP, STEPS, NO, N...]
where the time goes in v4:
time: 300 us
  Pallas kernels  298 us (99%)
    pallas_call x1, Pallas kernels, per_device(): pl.pallas_call(kernel, out_shape=jax.ShapeDtypeStruct((JUMP, STEPS, NO, N...  298 us

profile of v4, /device:TPU:1, one launch (start us, length us, event | category | flops | bytes accessed | tf_op | source)
XLA Modules:
  0.0 300.3 jit_solution(1763187337553529088)
XLA Ops:
  0.0 297.7 %shard_map.82 = bf16[4,3,256,256]{3,2,1,0:T(8,128)(2,1)} custom-call(bf16[4,3,256,256]{3,2,1,0:T(8,128)(2,1)} %bitcast.6, bf16[96,32,256]{2,1,0:T(8,128)(2,1)} %bitcast.7, bf16[4,3,2,256,256]{4,3,2,1,0:T(8,128)(2,1)} %bitcast.5, bf16[96,96]{1,0:T(8,128)(2,1)} %constant.10.clone.to_cells, bf16[96,96]{1,0:T(8,128)(2,1)} %constant.11.clone.to_points, ...), custom_call_target="tpu_custom_call" | custom-call | tf_op jit(solution)/shard_map/pallas_call | solution.py:414
  297.7 2.7 copy.10

commit v5 on v4

--- a/solution.py
+++ b/solution.py
@@ -218,44 +218,49 @@
         lax.fori_loop(0, SUB, lattice, 0, unroll=4)
         if turn:
             for s in range(STEPS):
-                take(sigma_in.at[0, s, pl.ds(0, TAU - 1)], sigma_sems.at[0, s, 0])
+                for uh in range(2):
+                    take(sigma_in.at[0, s, uh, pl.ds(0, TAU - 1)], sigma_sems.at[0, s, uh, 0])
                 take(dressed_in.at[0, s, pl.ds(0, KA - 1)], freq_sems.at[0, s, 0])
                 take(dressed_in.at[0, s, pl.ds(0, KA - 1)], dressed_sems.at[0, s, 0])
-                take(sigma_in.at[0, s, pl.ds(0, TAU - 1)], time_sems.at[0, s, 0])
+                take(time_in.at[0, s, pl.ds(0, TAU - 1)], time_sems.at[0, s, 0])
 
         for s in range(STEPS):
             for zh in range(2):
                 for uh in range(2):
                     rows, points = pl.ds(uh * 16, 16), pl.ds(zh * 16, 16)
-                    sigma_out[s, points, rows, :] = turn_over(swap, sigma[s, rows, points, :])
-
-            def part(d):
-                n, device = tau_peer(d)
-                send(sigma_out.at[s, n], sigma_in.at[turn, s, t], sigma_sems.at[turn, s], device)
-
-            loop(TAU, part)
-            sigma_in[turn, s, t] = sigma_out[s, t]
+                    sigma_out[s, uh, points] = turn_over(swap, sigma[s, rows, points, :])
+            for uh in range(2):
+
+                def part(d):
+                    n, device = tau_peer(d)
+                    send(
+                        sigma_out.at[s, uh, n], sigma_in.at[turn, s, uh, t],
+                        sigma_sems.at[turn, s, uh], device,
+                    )
+
+                loop(TAU, part)
+                sigma_in[turn, s, uh, t] = sigma_out[s, uh, t]
 
         def to_frequencies(s):
-            take(sigma_in.at[turn, s, pl.ds(0, TAU - 1)], sigma_sems.at[turn, s, 1])
-            for uh in range(2):
-                rows = pl.ds(uh * 16, 16)
-                block = sigma_in[turn, s, :, rows, :].reshape(512, NO)
-                value = mul(to_freq[...], block).astype(BF16)
-                freq_out[s, :, :, :, rows, :] = value.reshape(KA, 2, 2, 16, NO)
-
             def place(b):
                 return lax.rem(b // C + 2 * Y - my_j - s, Y) * C + lax.rem(b, C)
 
-            def part(d):
-                b, device = ka_peer(d)
-                send(
-                    freq_out.at[s, place(b)], freq_in.at[turn, s, :, :, my_rows, :],
-                    freq_sems.at[turn, s], device,
-                )
-
-            loop(KA, part)
-            freq_in[turn, s, :, :, my_rows, :] = freq_out[s, place(a)]
+            for uh in range(2):
+                take(sigma_in.at[turn, s, uh, pl.ds(0, TAU - 1)], sigma_sems.at[turn, s, uh, 1])
+                block = sigma_in[turn, s, uh].reshape(512, NO)
+                value = mul(to_freq[...], block).astype(BF16)
+                freq_out[s, uh] = value.reshape(KA, 2, 2, 16, NO)
+                rows = pl.ds(pl.multiple_of(a * SUB + uh * 16, 16), 16)
+
+                def part(d):
+                    b, device = ka_peer(d)
+                    send(
+                        freq_out.at[s, uh, place(b)], freq_in.at[turn, s, :, :, rows, :],
+                        freq_sems.at[turn, s], device,
+                    )
+
+                loop(KA, part)
+                freq_in[turn, s, :, :, rows, :] = freq_out[s, uh, place(a)]
 
         def solve(s):
             take(dressed_in.at[turn, s, pl.ds(0, KA - 1)], freq_sems.at[turn, s, 1])
@@ -307,7 +312,7 @@
             time_in[turn, s, t] = time_out[s, t]
 
         def finish(s):
-            take(sigma_in.at[turn, s, pl.ds(0, TAU - 1)], time_sems.at[turn, s, 1])
+            take(time_in.at[turn, s, pl.ds(0, TAU - 1)], time_sems.at[turn, s, 1])
 
             def place(b, j):
                 return (lax.rem(b, C) * JUMP + j) * X + lax.rem(b // C + j + s, X)
@@ -385,10 +390,11 @@
 
     for s in range(STEPS):
         take(x_parts.at[s, pl.ds(0, KA - 1)], x_sems.at[s, 0])
-        take(sigma_in.at[1, s, pl.ds(0, TAU - 1)], sigma_sems.at[1, s, 0])
+        for uh in range(2):
+            take(sigma_in.at[1, s, uh, pl.ds(0, TAU - 1)], sigma_sems.at[1, s, uh, 0])
         take(dressed_in.at[1, s, pl.ds(0, KA - 1)], freq_sems.at[1, s, 0])
         take(dressed_in.at[1, s, pl.ds(0, KA - 1)], dressed_sems.at[1, s, 0])
-        take(sigma_in.at[1, s, pl.ds(0, TAU - 1)], time_sems.at[1, s, 0])
+        take(time_in.at[1, s, pl.ds(0, TAU - 1)], time_sems.at[1, s, 0])
         for turn in range(2):
             take(x_parts.at[s, pl.ds(0, KA - 1)], home_sems.at[turn, s, 0])
         for j in range(JUMP):
@@ -422,9 +428,9 @@
             buffer(SUB, COUNT, NO),
             buffer(STEPS, SUB, TAU, NO),
             buffer(STEPS, SUB, TAU, NO),
-            buffer(STEPS, TAU, SUB, NO),
-            buffer(2, STEPS, TAU, SUB, NO),
-            buffer(STEPS, KA, 2, 2, SUB, NO),
+            buffer(STEPS, 2, TAU, 16, NO),
+            buffer(2, STEPS, 2, TAU, 16, NO),
+            buffer(STEPS, 2, KA, 2, 2, 16, NO),
             buffer(2, STEPS, 2, 2, NO, NO),
             buffer(STEPS, 2, 2, NO, NO),
             buffer(2, STEPS, KA, 2, 2, SUB, NO),
@@ -440,7 +446,7 @@
             dma(STEPS, 2),
             dma(STEPS, 2, 2),
             dma(STEPS, JUMP),
-            dma(2, STEPS, 2),
+            dma(2, STEPS, 2, 2),
             dma(2, STEPS, 2),
             dma(2, STEPS, 2),
             dma(2, STEPS, 2),

time: 300 us -> 298 us (level)
  Pallas kernels: 298 us -> 295 us
where the time goes in v5:
time: 298 us
  Pallas kernels  295 us (99%)
    pallas_call x1, Pallas kernels, per_device(): pl.pallas_call(kernel, out_shape=jax.ShapeDtypeStruct((JUMP, STEPS, NO, N...  295 us

profile of v5, /device:TPU:1, one launch (start us, length us, event | category | flops | bytes accessed | tf_op | source)
XLA Modules:
  0.0 297.7 jit_solution(10878088555236618915)
XLA Ops:
  0.0 295.1 %shard_map.82 = bf16[4,3,256,256]{3,2,1,0:T(8,128)(2,1)} custom-call(bf16[4,3,256,256]{3,2,1,0:T(8,128)(2,1)} %bitcast.6, bf16[96,32,256]{2,1,0:T(8,128)(2,1)} %bitcast.7, bf16[4,3,2,256,256]{4,3,2,1,0:T(8,128)(2,1)} %bitcast.5, bf16[96,96]{1,0:T(8,128)(2,1)} %constant.10.clone.to_cells, bf16[96,96]{1,0:T(8,128)(2,1)} %constant.11.clone.to_points, ...), custom_call_target="tpu_custom_call" | custom-call | tf_op jit(solution)/shard_map/pallas_call | solution.py:420
  295.1 2.7 copy.10

commit v6 on v5

--- a/solution.py
+++ b/solution.py
@@ -281,19 +281,19 @@
                 high_real, high_imag = dyson(br, bi, kr, ki)
                 dressed_out[s, i, 0] = (low_real - high_real).astype(BF16)
                 dressed_out[s, i, 1] = (low_imag + high_imag).astype(BF16)
+
+                def part(d):
+                    b, device = ka_peer(d)
+                    send(
+                        dressed_out.at[s, i, :, block_rows(b), :],
+                        dressed_in.at[turn, s, own_column(s) * C + my_c, i],
+                        dressed_sems.at[turn, s], device,
+                    )
+
+                loop(KA, part)
                 return c
 
             lax.fori_loop(0, 2, one, 0)
-            target = dressed_in.at[turn, s, own_column(s) * C + my_c]
-
-            def part(d):
-                b, device = ka_peer(d)
-                send(
-                    dressed_out.at[s, :, :, block_rows(b), :], target,
-                    dressed_sems.at[turn, s], device,
-                )
-
-            loop(KA, part)
             dressed_in[turn, s, own_column(s) * C + my_c] = dressed_out[s, :, :, my_rows, :]
 
         def to_times(s):

time: 298 us -> 295 us (0.990)
  Pallas kernels: 295 us -> 292 us
where the time goes in v6:
time: 295 us
  Pallas kernels  292 us (99%)
    pallas_call x1, Pallas kernels, per_device(): pl.pallas_call(kernel, out_shape=jax.ShapeDtypeStruct((JUMP, STEPS, NO, N...  292 us

profile of v6, /device:TPU:1, one launch (start us, length us, event | category | flops | bytes accessed | tf_op | source)
XLA Modules:
  0.0 294.9 jit_solution(7982343625023865145)
XLA Ops:
  0.0 292.2 %shard_map.82 = bf16[4,3,256,256]{3,2,1,0:T(8,128)(2,1)} custom-call(bf16[4,3,256,256]{3,2,1,0:T(8,128)(2,1)} %bitcast.6, bf16[96,32,256]{2,1,0:T(8,128)(2,1)} %bitcast.7, bf16[4,3,2,256,256]{4,3,2,1,0:T(8,128)(2,1)} %bitcast.5, bf16[96,96]{1,0:T(8,128)(2,1)} %constant.10.clone.to_cells, bf16[96,96]{1,0:T(8,128)(2,1)} %constant.11.clone.to_points, ...), custom_call_target="tpu_custom_call" | custom-call | tf_op jit(solution)/shard_map/pallas_call | solution.py:420
  292.2 2.7 copy.10
